TPU v7x, 32 devices: a whole 2x2x4 slice. The times are simulated.
32 devices in a mesh: blk: 8 (over z, y), dp: 4 (over x, core).
Axes of the slice: x: 2, y: 2, z: 4, core: 2. Of those that a mesh axis runs over, the one named last changes fastest.
Arguments:
- tokens: bfloat16 [4, 3072, 640], P('dp', 'blk'), may hold values from -6 to 6
- lengths: int32 [4, 4], P('dp'), may hold values from 0 to 3072, as said below
- cotangent: bfloat16 [4, 3072, 640], P('dp', 'blk'), may hold values from -6 to 6
- norm_in: float32 [640], replicated, may hold values from 0.1 to 1.9
- w_query: bfloat16 [640, 1024], replicated, may hold values from -0.25 to 0.25
- w_key: bfloat16 [640, 256], replicated, may hold values from -0.25 to 0.25
- w_value: bfloat16 [640, 256], replicated, may hold values from -0.25 to 0.25
- query_gain: float32 [256], replicated, may hold values from 0.1 to 1.9
- key_gain: float32 [256], replicated, may hold values from 0.1 to 1.9
- w_out: bfloat16 [1024, 640], replicated, may hold values from -0.1875 to 0.1875
- norm_attn: float32 [640], replicated, may hold values from 0.1 to 1.9
- norm_pre: float32 [640], replicated, may hold values from 0.1 to 1.9
- w_gate: bfloat16 [640, 2048], replicated, may hold values from -0.25 to 0.25
- w_up: bfloat16 [640, 2048], replicated, may hold values from -0.25 to 0.25
- w_down: bfloat16 [2048, 640], replicated, may hold values from -0.125 to 0.125
- norm_post: float32 [640], replicated, may hold values from 0.1 to 1.9
Outputs:
- output: bfloat16 [4, 3072, 640], P('dp', 'blk')
- input_grad: bfloat16 [4, 3072, 640], P('dp', 'blk')
- grad_norm_in: float32 [640], replicated
- grad_query: float32 [640, 1024], replicated
- grad_key: float32 [640, 256], replicated
- grad_value: float32 [640, 256], replicated
- grad_query_gain: float32 [256], replicated
- grad_key_gain: float32 [256], replicated
- grad_out: float32 [1024, 640], replicated
- grad_norm_attn: float32 [640], replicated
- grad_norm_pre: float32 [640], replicated
- grad_gate: float32 [640, 2048], replicated
- grad_up: float32 [640, 2048], replicated
- grad_down: float32 [2048, 640], replicated
- grad_norm_post: float32 [640], replicated
Inputs may be any that keep to these rules, and one draw needn't show every extreme that they name: Each row holds the lengths of a group's sequences in order, summing to 3072: one, two or four positive lengths followed by zeros; some group in every draw is a single sequence of 3072 tokens.
All inputs are finite; a program needn't handle non-finite values.
Results may differ from a plain program's by a relative error of at most 0.025.
Values may be sent and summed in bfloat16 or wider, within the bound.
A program may use at most 192 MiB of HBM per device.

v0:
```python
import jax
import jax.numpy as jnp
from jax import lax
from jax.sharding import PartitionSpec as P

EPS = 1e-06
BASE = 1000000.0
NEG = -1e30


def shifted(array, axis, by):
    peers = lax.axis_size(axis)
    return lax.ppermute(array, axis, [(i, (i + by) % peers) for i in range(peers)])


def from_behind(block, axis, distance):
    devices = range(lax.axis_size(axis))
    route = [(i - distance, i) for i in devices if i - distance in devices]
    return lax.ppermute(block, axis, route)


def normed(value, gain):
    return value * lax.rsqrt(jnp.mean(value * value, axis=-1, keepdims=True) + EPS) * gain


def normed_back(value, gain, grad):
    return jax.vjp(normed, value, gain)[1](grad)


def segment_of(index, row):
    ends = jnp.cumsum(row)
    seg = jnp.sum((index[:, None] >= ends[None, :]).astype(jnp.int32), axis=1)
    starts = ends - row
    slots = jnp.arange(row.shape[0], dtype=jnp.int32)
    begin = jnp.sum(jnp.where(slots[None, :] == seg[:, None], starts[None, :], 0), axis=1)
    return (seg, index - begin)


def rotary_tables(places, head):
    half = head // 2
    freq = jnp.exp(-(2.0 * jnp.arange(half, dtype=jnp.float32) / head) * jnp.log(BASE))
    angle = places.astype(jnp.float32)[:, None] * freq[None, :]
    return (jnp.cos(angle), jnp.sin(angle))


def prepare(proj, gain, cosine, sine):
    value = normed(proj, gain)
    half = value.shape[-1] // 2
    first = value[..., :half]
    second = value[..., half:]
    return jnp.concatenate(
        [first * cosine - second * sine, second * cosine + first * sine], axis=-1
    )


def pass_home(grads):
    return shifted(grads.astype(jnp.bfloat16), "blk", 1).astype(grads.dtype)


def per_device(
    tokens,
    lengths,
    cotangent,
    norm_in,
    w_query,
    w_key,
    w_value,
    query_gain,
    key_gain,
    w_out,
    norm_attn,
    norm_pre,
    w_gate,
    w_up,
    w_down,
    norm_post,
):
    rows = tokens.shape[1]
    head = query_gain.shape[0]
    heads = w_query.shape[1] // head
    scale = head ** (-0.5)
    count = lax.axis_size("blk")
    place = lax.axis_index("blk")
    row = lengths[0]
    local_idx = place * rows + jnp.arange(rows, dtype=jnp.int32)
    seg_q, pos_q = segment_of(local_idx, row)
    cosine, sine = rotary_tables(pos_q, head)

    def block_mask(source):
        key_idx = source * rows + jnp.arange(rows, dtype=jnp.int32)
        seg_k, unused = segment_of(key_idx, row)
        return (seg_q[:, None] == seg_k[None, :]) & (local_idx[:, None] >= key_idx[None, :])

    x_in = tokens[0].astype(jnp.float32)
    normal_a = normed(x_in, norm_in).astype(jnp.bfloat16)
    q_proj = jnp.dot(normal_a, w_query, preferred_element_type=jnp.float32).reshape(
        rows, heads, head
    )
    k_proj = jnp.dot(normal_a, w_key, preferred_element_type=jnp.float32)
    v_proj = jnp.dot(normal_a, w_value, preferred_element_type=jnp.float32)
    query = prepare(q_proj, query_gain, cosine[:, None, :], sine[:, None, :]).astype(jnp.bfloat16)
    keys = prepare(k_proj, key_gain, cosine, sine).astype(jnp.bfloat16)
    values = v_proj.astype(jnp.bfloat16)
    q_heads = jnp.transpose(query, (1, 0, 2))

    def absorb(state, pair, source):
        allowed = block_mask(source)
        big, total, accum = state
        raw = jnp.einsum("hqd,kd->hqk", q_heads, pair[0], preferred_element_type=jnp.float32)
        scores = jnp.where(allowed[None], scale * raw, NEG)
        big_new = jnp.maximum(big, jnp.max(scores, axis=-1, keepdims=True))
        expo = jnp.where(allowed[None], jnp.exp(scores - big_new), 0.0)
        fade = jnp.exp(big - big_new)
        total = total * fade + jnp.sum(expo, axis=-1, keepdims=True)
        accum = accum * fade + jnp.einsum(
            "hqk,kd->hqd", expo.astype(jnp.bfloat16), pair[1], preferred_element_type=jnp.float32
        )
        return (big_new, total, accum)

    pair = jnp.stack([keys, values])
    state = (
        jnp.full((heads, rows, 1), NEG, jnp.float32),
        jnp.zeros((heads, rows, 1), jnp.float32),
        jnp.zeros((heads, rows, head), jnp.float32),
    )
    state = absorb(state, pair, place)

    def cycle_forward(step, carry):
        inner, moving = carry
        moving = from_behind(moving, "blk", 1)
        return (absorb(inner, moving, (place - step) % count), moving)

    state, unused_pair = lax.fori_loop(1, count, cycle_forward, (state, pair))
    big, total, accum = state
    attended = accum / total
    lse = big + jnp.log(total)
    joined = jnp.transpose(attended, (1, 0, 2)).reshape(rows, heads * head).astype(jnp.bfloat16)
    a_proj = jnp.dot(joined, w_out, preferred_element_type=jnp.float32)
    x_mid = x_in + normed(a_proj, norm_attn)
    mixed = normed(x_mid, norm_pre).astype(jnp.bfloat16)
    gate = jnp.dot(mixed, w_gate, preferred_element_type=jnp.float32)
    upper = jnp.dot(mixed, w_up, preferred_element_type=jnp.float32)

    def activate(gate_in, upper_in):
        return jax.nn.gelu(gate_in, approximate=True) * upper_in

    hidden = activate(gate, upper).astype(jnp.bfloat16)
    f_proj = jnp.dot(hidden, w_down, preferred_element_type=jnp.float32)
    output = x_mid + normed(f_proj, norm_post)
    grad_y = cotangent[0].astype(jnp.float32)
    d_fproj, g_post = normed_back(f_proj, norm_post, grad_y)
    d_fproj = d_fproj.astype(jnp.bfloat16)
    g_down = jnp.einsum("tf,td->fd", hidden, d_fproj, preferred_element_type=jnp.float32)
    d_hidden = jnp.einsum("td,fd->tf", d_fproj, w_down, preferred_element_type=jnp.float32)
    d_gate, d_upper = jax.vjp(activate, gate, upper)[1](d_hidden)
    d_gate = d_gate.astype(jnp.bfloat16)
    d_upper = d_upper.astype(jnp.bfloat16)
    g_gate = jnp.einsum("td,tf->df", mixed, d_gate, preferred_element_type=jnp.float32)
    g_up = jnp.einsum("td,tf->df", mixed, d_upper, preferred_element_type=jnp.float32)
    d_mixed = jnp.einsum(
        "tf,df->td", d_gate, w_gate, preferred_element_type=jnp.float32
    ) + jnp.einsum("tf,df->td", d_upper, w_up, preferred_element_type=jnp.float32)
    d_mid, g_pre = normed_back(x_mid, norm_pre, d_mixed)
    d_mid = grad_y + d_mid
    d_aproj, g_attn = normed_back(a_proj, norm_attn, d_mid)
    d_aproj = d_aproj.astype(jnp.bfloat16)
    g_out = jnp.einsum("tn,td->nd", joined, d_aproj, preferred_element_type=jnp.float32)
    d_joined = jnp.einsum("td,nd->tn", d_aproj, w_out, preferred_element_type=jnp.float32).astype(
        jnp.bfloat16
    )
    do_heads = jnp.transpose(d_joined.reshape(rows, heads, head), (1, 0, 2))
    delta = jnp.sum(do_heads.astype(jnp.float32) * attended, axis=-1, keepdims=True)

    def visit(d_query, moving, grads, source):
        allowed = block_mask(source)
        raw = jnp.einsum("hqd,kd->hqk", q_heads, moving[0], preferred_element_type=jnp.float32)
        probs = jnp.where(allowed[None], jnp.exp(scale * raw - lse), 0.0)
        dv_add = jnp.einsum(
            "hqk,hqd->kd", probs.astype(jnp.bfloat16), do_heads, preferred_element_type=jnp.float32
        )
        d_probs = jnp.einsum("hqd,kd->hqk", do_heads, moving[1], preferred_element_type=jnp.float32)
        d_scores = (scale * probs * (d_probs - delta)).astype(jnp.bfloat16)
        dq_add = jnp.einsum("hqk,kd->hqd", d_scores, moving[0], preferred_element_type=jnp.float32)
        dk_add = jnp.einsum("hqk,hqd->kd", d_scores, q_heads, preferred_element_type=jnp.float32)
        return (d_query + dq_add, grads + jnp.stack([dk_add, dv_add]))

    d_query = jnp.zeros((heads, rows, head), jnp.float32)
    grads = jnp.zeros((2, rows, head), jnp.float32)
    d_query, grads = visit(d_query, pair, grads, place)

    def cycle_backward(step, carry):
        dq_in, moving, grads_in = carry
        moving = from_behind(moving, "blk", 1)
        grads_in = pass_home(grads_in)
        dq_in, grads_in = visit(dq_in, moving, grads_in, (place - step) % count)
        return (dq_in, moving, grads_in)

    d_query, unused_pair, grads = lax.fori_loop(1, count, cycle_backward, (d_query, pair, grads))
    grads = pass_home(grads)

    def query_piece(proj, gain):
        return prepare(proj, gain, cosine[:, None, :], sine[:, None, :])

    def key_piece(proj, gain):
        return prepare(proj, gain, cosine, sine)

    d_qproj, g_qgain = jax.vjp(query_piece, q_proj, query_gain)[1](
        jnp.transpose(d_query, (1, 0, 2))
    )
    d_kproj, g_kgain = jax.vjp(key_piece, k_proj, key_gain)[1](grads[0])
    d_qproj = d_qproj.reshape(rows, heads * head).astype(jnp.bfloat16)
    d_kproj = d_kproj.astype(jnp.bfloat16)
    d_vproj = grads[1].astype(jnp.bfloat16)
    g_query = jnp.einsum("td,tn->dn", normal_a, d_qproj, preferred_element_type=jnp.float32)
    g_key = jnp.einsum("td,tn->dn", normal_a, d_kproj, preferred_element_type=jnp.float32)
    g_value = jnp.einsum("td,tn->dn", normal_a, d_vproj, preferred_element_type=jnp.float32)
    d_normal = jnp.einsum("tn,dn->td", d_qproj, w_query, preferred_element_type=jnp.float32)
    d_normal = d_normal + jnp.einsum(
        "tn,dn->td", d_kproj, w_key, preferred_element_type=jnp.float32
    )
    d_normal = d_normal + jnp.einsum(
        "tn,dn->td", d_vproj, w_value, preferred_element_type=jnp.float32
    )
    d_input, g_in = normed_back(x_in, norm_in, d_normal)
    input_grad = (d_mid + d_input).astype(jnp.bfloat16)
    (
        g_in,
        g_query,
        g_key,
        g_value,
        g_qgain,
        g_kgain,
        g_out,
        g_attn,
        g_pre,
        g_gate,
        g_up,
        g_down,
        g_post,
    ) = lax.psum(
        (
            g_in,
            g_query,
            g_key,
            g_value,
            g_qgain,
            g_kgain,
            g_out,
            g_attn,
            g_pre,
            g_gate,
            g_up,
            g_down,
            g_post,
        ),
        ("blk", "dp"),
    )
    return (
        output.astype(jnp.bfloat16)[None],
        input_grad[None],
        g_in,
        g_query,
        g_key,
        g_value,
        g_qgain,
        g_kgain,
        g_out,
        g_attn,
        g_pre,
        g_gate,
        g_up,
        g_down,
        g_post,
    )


def solution(mesh):
    in_specs = (
        P("dp", "blk", None),
        P("dp", None),
        P("dp", "blk", None),
        P(),
        P(),
        P(),
        P(),
        P(),
        P(),
        P(),
        P(),
        P(),
        P(),
        P(),
        P(),
        P(),
    )
    out_specs = (
        P("dp", "blk", None),
        P("dp", "blk", None),
        P(),
        P(),
        P(),
        P(),
        P(),
        P(),
        P(),
        P(),
        P(),
        P(),
        P(),
        P(),
        P(),
    )
    return jax.shard_map(
        per_device, mesh=mesh, in_specs=in_specs, out_specs=out_specs, check_vma=False
    )
```

profile of v0, /device:TPU:0, one launch (start us, length us, event | category | flops | bytes accessed | tf_op | source)
XLA Modules:
  0.0 782.4 jit_solution(8812771186704844090)
XLA Ops:
  36.1 132.0 %while.42 = (s32[]{:T(128)}, f32[4,384,1]{1,0,2:T(4,128)S(1)}, f32[4,384,1]{1,0,2:T(4,128)S(1)}, f32[4,384,256]{2,1,0:T(8,128)}, bf16[2,384,256]{2,1,0:T(8,128)(...) while((s32[]{:T(128)}, f32[4,384,1]{1,0,2:T(4,128)S(1)}, ...), condition=%wide.region_13.14_spmd.clone, body=%wide.region_9.13_spmd.clone.sunk | while | flops 612885888 | bytes 27046280 | solution.py:133
  36.1 5.6 collective-permute-start
  42.0 7.6 collective-permute-done
  56.9 5.1 collective-permute-start
  62.3 6.8 collective-permute-done
  76.4 5.1 collective-permute-start
  81.8 5.9 collective-permute-done
  95.0 5.9 collective-permute-start
  101.2 4.9 collective-permute-done
  113.4 6.0 collective-permute-start
  131.6 6.0 collective-permute-start
  149.8 6.0 collective-permute-start
  204.0 147.1 %while.43 = (s32[]{:T(128)}, f32[4,384,256]{2,1,0:T(8,128)S(1)}, bf16[2,384,256]{2,1,0:T(8,128)(2,1)}, bf16[2,384,256]{2,1,0:T(8,128)(2,1)}, s32[384]{0:T(512)S(...) while((s32[]{:T(128)}, f32[4,384,256]{2,1,0:T(8,128)S(1)}, ...), condition=%wide.region_23.24_spmd.clone, body=%wide.region_21.23_spmd.clone.sunk | while | flops 1518064512 | bytes 27408804 | solution.py:198
  207.4 5.3 collective-permute-start.1
  213.0 5.2 collective-permute-done.1
  226.4 5.2 collective-permute-start.1
  231.9 5.8 collective-permute-done.1
  250.6 7.0 collective-permute-done.1
  270.4 8.1 %collective-permute-done.1 = bf16[2,384,256]{2,1,0:T(8,128)(2,1)S(1)} collective-permute-done((bf16[2,384,256]{2,1,0:T(8,128)(2,1)}, bf16[2,384,256]{2,1,0:T(8,128)(2,1)S(1)}, u32[]{:S(2)}, u32[]{:S(2)}) %collective-permute-start.1) | collective-permute-done | bytes 393248 | tf_op jit(solution)/shard_map/while/body/eval_jaxpr/ppermute | solution.py:19
  291.3 9.2 %collective-permute-done.1 = bf16[2,384,256]{2,1,0:T(8,128)(2,1)S(1)} collective-permute-done((bf16[2,384,256]{2,1,0:T(8,128)(2,1)}, bf16[2,384,256]{2,1,0:T(8,128)(2,1)S(1)}, u32[]{:S(2)}, u32[]{:S(2)}) %collective-permute-start.1) | collective-permute-done | bytes 393248 | tf_op jit(solution)/shard_map/while/body/eval_jaxpr/ppermute | solution.py:19
  313.3 9.8 %collective-permute-done.1 = bf16[2,384,256]{2,1,0:T(8,128)(2,1)S(1)} collective-permute-done((bf16[2,384,256]{2,1,0:T(8,128)(2,1)}, bf16[2,384,256]{2,1,0:T(8,128)(2,1)S(1)}, u32[]{:S(2)}, u32[]{:S(2)}) %collective-permute-start.1) | collective-permute-done | bytes 393248 | tf_op jit(solution)/shard_map/while/body/eval_jaxpr/ppermute | solution.py:19
  336.3 9.2 %collective-permute-done.1 = bf16[2,384,256]{2,1,0:T(8,128)(2,1)S(1)} collective-permute-done((bf16[2,384,256]{2,1,0:T(8,128)(2,1)}, bf16[2,384,256]{2,1,0:T(8,128)(2,1)S(1)}, u32[]{:S(2)}, u32[]{:S(2)}) %collective-permute-start.1) | collective-permute-done | bytes 393248 | tf_op jit(solution)/shard_map/while/body/eval_jaxpr/ppermute | solution.py:19
  387.2 43.7 %all-reduce.4 = (f32[640]{0:T(1024)}, f32[256]{0:T(256)}, f32[256]{0:T(256)}, f32[640]{0:T(1024)}, f32[640]{0:T(1024)}, /*index=5*/f32[640]{0:T(1024)}) all-reduce(f32[640]{0:T(1024)S(1)} %get-tuple-element.681, f32[256]{0:T(256)S(1)} %get-tuple-element.673, ...), channel_id=1, replica_groups=mesh['blk'=8,'dp'=4] {'blk','dp'}, use_global_device_ids=true, to_apply=%region_28.29 | all-reduce | flops 3072 | bytes 24576 | tf_op jit(solution)/shard_map/psum | solution.py:240
  432.1 323.8 %all-reduce.8.cloned.1.call-done = (f32[640,1024]{1,0:T(8,128)}, f32[640,256]{1,0:T(8,128)}, f32[640,256]{1,0:T(8,128)}, f32[1024,640]{1,0:T(8,128)}, f32[640,20...) async-done(((f32[640,1024]{1,0:T(8,128)}, f32[640,256]{1,0:T(8,128)}, f32[640,256]{1,0:T(8,128)}, f32[1024,640]{1,0:T(8,128)}, f32[640,2048]{1,0:T(8,128)}, ...) | async-done | bytes 22282256 | tf_op jit(solution)/shard_map/psum | solution.py:240
  (462 shorter events, 268.4 us)
Async XLA Ops:
  7.2 170.2 %copy-start = (bf16[640,2048]{1,0:T(8,128)(2,1)S(1)}, bf16[640,2048]{1,0:T(8,128)(2,1)}, u32[]{:S(2)}) copy-start(bf16[640,2048]{1,0:T(8,128)(2,1)} %param.33) | copy-start | bytes 7864324
  7.2 748.6 %all-reduce.8.cloned.1.call-start = ((), (), s32[]{:S(2)}) async-start(), calls=%async_computation | async-start | bytes 44564480 | tf_op jit(solution)/shard_map/psum | solution.py:240
  36.1 13.5 %collective-permute-start = (bf16[2,384,256]{2,1,0:T(8,128)(2,1)}, bf16[2,384,256]{2,1,0:T(8,128)(2,1)}, u32[]{:S(2)}, u32[]{:S(2)}) collective-permute-start(bf16[2,384,256]{2,1,0:T(8,128)(2,1)} %get-tuple-element.949), channel_id=1, source_target_pairs={{0,4},{4,8},{8,12},{12,16},{16,20},{20,24},{24,28},{1,5},{5,9},{9,... | collective-permute-start | bytes 1179656 | tf_op jit(solution)/shard_map/while/body/eval_jaxpr/ppermute | solution.py:19
  56.9 12.2 %collective-permute-start = (bf16[2,384,256]{2,1,0:T(8,128)(2,1)}, bf16[2,384,256]{2,1,0:T(8,128)(2,1)}, u32[]{:S(2)}, u32[]{:S(2)}) collective-permute-start(bf16[2,384,256]{2,1,0:T(8,128)(2,1)} %get-tuple-element.949), channel_id=1, source_target_pairs={{0,4},{4,8},{8,12},{12,16},{16,20},{20,24},{24,28},{1,5},{5,9},{9,... | collective-permute-start | bytes 1179656 | tf_op jit(solution)/shard_map/while/body/eval_jaxpr/ppermute | solution.py:19
  76.4 11.3 %collective-permute-start = (bf16[2,384,256]{2,1,0:T(8,128)(2,1)}, bf16[2,384,256]{2,1,0:T(8,128)(2,1)}, u32[]{:S(2)}, u32[]{:S(2)}) collective-permute-start(bf16[2,384,256]{2,1,0:T(8,128)(2,1)} %get-tuple-element.949), channel_id=1, source_target_pairs={{0,4},{4,8},{8,12},{12,16},{16,20},{20,24},{24,28},{1,5},{5,9},{9,... | collective-permute-start | bytes 1179656 | tf_op jit(solution)/shard_map/while/body/eval_jaxpr/ppermute | solution.py:19
  95.0 11.1 %collective-permute-start = (bf16[2,384,256]{2,1,0:T(8,128)(2,1)}, bf16[2,384,256]{2,1,0:T(8,128)(2,1)}, u32[]{:S(2)}, u32[]{:S(2)}) collective-permute-start(bf16[2,384,256]{2,1,0:T(8,128)(2,1)} %get-tuple-element.949), channel_id=1, source_target_pairs={{0,4},{4,8},{8,12},{12,16},{16,20},{20,24},{24,28},{1,5},{5,9},{9,... | collective-permute-start | bytes 1179656 | tf_op jit(solution)/shard_map/while/body/eval_jaxpr/ppermute | solution.py:19
  113.4 10.9 %collective-permute-start = (bf16[2,384,256]{2,1,0:T(8,128)(2,1)}, bf16[2,384,256]{2,1,0:T(8,128)(2,1)}, u32[]{:S(2)}, u32[]{:S(2)}) collective-permute-start(bf16[2,384,256]{2,1,0:T(8,128)(2,1)} %get-tuple-element.949), channel_id=1, source_target_pairs={{0,4},{4,8},{8,12},{12,16},{16,20},{20,24},{24,28},{1,5},{5,9},{9,... | collective-permute-start | bytes 1179656 | tf_op jit(solution)/shard_map/while/body/eval_jaxpr/ppermute | solution.py:19
  131.6 10.9 %collective-permute-start = (bf16[2,384,256]{2,1,0:T(8,128)(2,1)}, bf16[2,384,256]{2,1,0:T(8,128)(2,1)}, u32[]{:S(2)}, u32[]{:S(2)}) collective-permute-start(bf16[2,384,256]{2,1,0:T(8,128)(2,1)} %get-tuple-element.949), channel_id=1, source_target_pairs={{0,4},{4,8},{8,12},{12,16},{16,20},{20,24},{24,28},{1,5},{5,9},{9,... | collective-permute-start | bytes 1179656 | tf_op jit(solution)/shard_map/while/body/eval_jaxpr/ppermute | solution.py:19
  149.8 10.9 %collective-permute-start = (bf16[2,384,256]{2,1,0:T(8,128)(2,1)}, bf16[2,384,256]{2,1,0:T(8,128)(2,1)}, u32[]{:S(2)}, u32[]{:S(2)}) collective-permute-start(bf16[2,384,256]{2,1,0:T(8,128)(2,1)} %get-tuple-element.949), channel_id=1, source_target_pairs={{0,4},{4,8},{8,12},{12,16},{16,20},{20,24},{24,28},{1,5},{5,9},{9,... | collective-permute-start | bytes 1179656 | tf_op jit(solution)/shard_map/while/body/eval_jaxpr/ppermute | solution.py:19
  204.0 19.0 %collective-permute-start.2 = (bf16[2,384,256]{2,1,0:T(8,128)(2,1)}, bf16[2,384,256]{2,1,0:T(8,128)(2,1)S(1)}, u32[]{:S(2)}, u32[]{:S(2)}) collective-permute-start(bf16[2,384,256]{2,1,0:T(8,128)(2,1)} %get-tuple-element.995), channel_id=1, source_target_pairs={{0,4},{4,8},{8,12},{12,16},{16,20},{20,24},{24,28},{28,0},{1,5},{5... | collective-permute-start | bytes 1179656 | tf_op jit(solution)/shard_map/while/body/eval_jaxpr/ppermute | solution.py:13
  207.4 10.9 %collective-permute-start.1 = (bf16[2,384,256]{2,1,0:T(8,128)(2,1)}, bf16[2,384,256]{2,1,0:T(8,128)(2,1)S(1)}, u32[]{:S(2)}, u32[]{:S(2)}) collective-permute-start(bf16[2,384,256]{2,1,0:T(8,128)(2,1)} %get-tuple-element.994), channel_id=1, source_target_pairs={{0,4},{4,8},{8,12},{12,16},{16,20},{20,24},{24,28},{1,5},{5,9},{9,... | collective-permute-start | bytes 1179656 | tf_op jit(solution)/shard_map/while/body/eval_jaxpr/ppermute | solution.py:19
  223.9 18.6 %collective-permute-start.2 = (bf16[2,384,256]{2,1,0:T(8,128)(2,1)}, bf16[2,384,256]{2,1,0:T(8,128)(2,1)S(1)}, u32[]{:S(2)}, u32[]{:S(2)}) collective-permute-start(bf16[2,384,256]{2,1,0:T(8,128)(2,1)} %get-tuple-element.995), channel_id=1, source_target_pairs={{0,4},{4,8},{8,12},{12,16},{16,20},{20,24},{24,28},{28,0},{1,5},{5... | collective-permute-start | bytes 1179656 | tf_op jit(solution)/shard_map/while/body/eval_jaxpr/ppermute | solution.py:13
  226.4 11.4 %collective-permute-start.1 = (bf16[2,384,256]{2,1,0:T(8,128)(2,1)}, bf16[2,384,256]{2,1,0:T(8,128)(2,1)S(1)}, u32[]{:S(2)}, u32[]{:S(2)}) collective-permute-start(bf16[2,384,256]{2,1,0:T(8,128)(2,1)} %get-tuple-element.994), channel_id=1, source_target_pairs={{0,4},{4,8},{8,12},{12,16},{16,20},{20,24},{24,28},{1,5},{5,9},{9,... | collective-permute-start | bytes 1179656 | tf_op jit(solution)/shard_map/while/body/eval_jaxpr/ppermute | solution.py:19
  243.4 19.0 %collective-permute-start.2 = (bf16[2,384,256]{2,1,0:T(8,128)(2,1)}, bf16[2,384,256]{2,1,0:T(8,128)(2,1)S(1)}, u32[]{:S(2)}, u32[]{:S(2)}) collective-permute-start(bf16[2,384,256]{2,1,0:T(8,128)(2,1)} %get-tuple-element.995), channel_id=1, source_target_pairs={{0,4},{4,8},{8,12},{12,16},{16,20},{20,24},{24,28},{28,0},{1,5},{5... | collective-permute-start | bytes 1179656 | tf_op jit(solution)/shard_map/while/body/eval_jaxpr/ppermute | solution.py:13
  245.8 11.9 %collective-permute-start.1 = (bf16[2,384,256]{2,1,0:T(8,128)(2,1)}, bf16[2,384,256]{2,1,0:T(8,128)(2,1)S(1)}, u32[]{:S(2)}, u32[]{:S(2)}) collective-permute-start(bf16[2,384,256]{2,1,0:T(8,128)(2,1)} %get-tuple-element.994), channel_id=1, source_target_pairs={{0,4},{4,8},{8,12},{12,16},{16,20},{20,24},{24,28},{1,5},{5,9},{9,... | collective-permute-start | bytes 1179656 | tf_op jit(solution)/shard_map/while/body/eval_jaxpr/ppermute | solution.py:19
  263.2 20.0 %collective-permute-start.2 = (bf16[2,384,256]{2,1,0:T(8,128)(2,1)}, bf16[2,384,256]{2,1,0:T(8,128)(2,1)S(1)}, u32[]{:S(2)}, u32[]{:S(2)}) collective-permute-start(bf16[2,384,256]{2,1,0:T(8,128)(2,1)} %get-tuple-element.995), channel_id=1, source_target_pairs={{0,4},{4,8},{8,12},{12,16},{16,20},{20,24},{24,28},{28,0},{1,5},{5... | collective-permute-start | bytes 1179656 | tf_op jit(solution)/shard_map/while/body/eval_jaxpr/ppermute | solution.py:13
  265.6 12.9 %collective-permute-start.1 = (bf16[2,384,256]{2,1,0:T(8,128)(2,1)}, bf16[2,384,256]{2,1,0:T(8,128)(2,1)S(1)}, u32[]{:S(2)}, u32[]{:S(2)}) collective-permute-start(bf16[2,384,256]{2,1,0:T(8,128)(2,1)} %get-tuple-element.994), channel_id=1, source_target_pairs={{0,4},{4,8},{8,12},{12,16},{16,20},{20,24},{24,28},{1,5},{5,9},{9,... | collective-permute-start | bytes 1179656 | tf_op jit(solution)/shard_map/while/body/eval_jaxpr/ppermute | solution.py:19
  284.1 21.1 %collective-permute-start.2 = (bf16[2,384,256]{2,1,0:T(8,128)(2,1)}, bf16[2,384,256]{2,1,0:T(8,128)(2,1)S(1)}, u32[]{:S(2)}, u32[]{:S(2)}) collective-permute-start(bf16[2,384,256]{2,1,0:T(8,128)(2,1)} %get-tuple-element.995), channel_id=1, source_target_pairs={{0,4},{4,8},{8,12},{12,16},{16,20},{20,24},{24,28},{28,0},{1,5},{5... | collective-permute-start | bytes 1179656 | tf_op jit(solution)/shard_map/while/body/eval_jaxpr/ppermute | solution.py:13
  286.5 14.0 %collective-permute-start.1 = (bf16[2,384,256]{2,1,0:T(8,128)(2,1)}, bf16[2,384,256]{2,1,0:T(8,128)(2,1)S(1)}, u32[]{:S(2)}, u32[]{:S(2)}) collective-permute-start(bf16[2,384,256]{2,1,0:T(8,128)(2,1)} %get-tuple-element.994), channel_id=1, source_target_pairs={{0,4},{4,8},{8,12},{12,16},{16,20},{20,24},{24,28},{1,5},{5,9},{9,... | collective-permute-start | bytes 1179656 | tf_op jit(solution)/shard_map/while/body/eval_jaxpr/ppermute | solution.py:19
  306.1 21.7 %collective-permute-start.2 = (bf16[2,384,256]{2,1,0:T(8,128)(2,1)}, bf16[2,384,256]{2,1,0:T(8,128)(2,1)S(1)}, u32[]{:S(2)}, u32[]{:S(2)}) collective-permute-start(bf16[2,384,256]{2,1,0:T(8,128)(2,1)} %get-tuple-element.995), channel_id=1, source_target_pairs={{0,4},{4,8},{8,12},{12,16},{16,20},{20,24},{24,28},{28,0},{1,5},{5... | collective-permute-start | bytes 1179656 | tf_op jit(solution)/shard_map/while/body/eval_jaxpr/ppermute | solution.py:13
  308.5 14.6 %collective-permute-start.1 = (bf16[2,384,256]{2,1,0:T(8,128)(2,1)}, bf16[2,384,256]{2,1,0:T(8,128)(2,1)S(1)}, u32[]{:S(2)}, u32[]{:S(2)}) collective-permute-start(bf16[2,384,256]{2,1,0:T(8,128)(2,1)} %get-tuple-element.994), channel_id=1, source_target_pairs={{0,4},{4,8},{8,12},{12,16},{16,20},{20,24},{24,28},{1,5},{5,9},{9,... | collective-permute-start | bytes 1179656 | tf_op jit(solution)/shard_map/while/body/eval_jaxpr/ppermute | solution.py:19
  328.7 21.5 %collective-permute-start.2 = (bf16[2,384,256]{2,1,0:T(8,128)(2,1)}, bf16[2,384,256]{2,1,0:T(8,128)(2,1)S(1)}, u32[]{:S(2)}, u32[]{:S(2)}) collective-permute-start(bf16[2,384,256]{2,1,0:T(8,128)(2,1)} %get-tuple-element.995), channel_id=1, source_target_pairs={{0,4},{4,8},{8,12},{12,16},{16,20},{20,24},{24,28},{28,0},{1,5},{5... | collective-permute-start | bytes 1179656 | tf_op jit(solution)/shard_map/while/body/eval_jaxpr/ppermute | solution.py:13
  331.1 14.4 %collective-permute-start.1 = (bf16[2,384,256]{2,1,0:T(8,128)(2,1)}, bf16[2,384,256]{2,1,0:T(8,128)(2,1)S(1)}, u32[]{:S(2)}, u32[]{:S(2)}) collective-permute-start(bf16[2,384,256]{2,1,0:T(8,128)(2,1)} %get-tuple-element.994), channel_id=1, source_target_pairs={{0,4},{4,8},{8,12},{12,16},{16,20},{20,24},{24,28},{1,5},{5,9},{9,... | collective-permute-start | bytes 1179656 | tf_op jit(solution)/shard_map/while/body/eval_jaxpr/ppermute | solution.py:19
  353.1 25.8 %collective-permute-start.3 = (bf16[2,384,256]{1,2,0:T(8,128)(2,1)}, bf16[2,384,256]{1,2,0:T(8,128)(2,1)}, u32[]{:S(2)}, u32[]{:S(2)}) collective-permute-start(bf16[2,384,256]{1,2,0:T(8,128)(2,1)} %copy.101), channel_id=1, source_target_pairs={{0,4},{4,8},{8,12},{12,16},{16,20},{20,24},{24,28},{28,0},{1,5},{5... | collective-permute-start | bytes 1179656 | tf_op jit(solution)/shard_map/ppermute | solution.py:13
  (96 other events, 386.1 us)
Sparse Core Ops, SparseCore 0:
  383.9 371.8 all-reduce.7
where the time goes:
time: 791 us; the launch traced here: 782 us
  waiting for transfers between devices  417 us (53%)
  matrix products  106 us (13%)
  starting transfers between devices  93.6 us (12%)
  local copies, waits for them, and re-layouts  69.2 us (9%)
  blocking collectives  43.7 us (6%)
  other arithmetic  36.3 us (5%)
  between operations  15.4 us (2%)
    psum x1, waiting for transfers between devices, per_device(): lax.psum((g_in, g_query, g_key, g_value, g_qgain, g_kgain, g_out, g_attn,...  324 us
    ppermute x14, waiting for transfers between devices, from_behind(): return lax.ppermute(block, axis, route)  93.3 us
    ppermute x14, starting transfers between devices, from_behind(): return lax.ppermute(block, axis, route)  73.2 us
    psum x1, blocking collectives, per_device(): lax.psum((g_in, g_query, g_key, g_value, g_qgain, g_kgain, g_out, g_attn,...  43.7 us
    unnamed x163, local copies, waits for them, and re-layouts  32.9 us
    while x63, local copies, waits for them, and re-layouts  25.7 us
    ppermute x8, starting transfers between devices, shifted(): lax.ppermute(array, axis, [(i, (i + by) % peers) for i in range(peers)])  20.4 us
    dot_general x8, matrix products, absorb(): jnp.einsum('hqk,kd->hqd', expo.astype(jnp.bfloat16), pair[1], preferred_e...  17.7 us
  transfers between devices with their start and end apart: 23, of which 15 were waited for; matrix products, arithmetic and copies ran while one was open for 8% of the time, Pallas kernels for 0%

commit v1 on v0

--- a/solution.py
+++ b/solution.py
@@ -1,6 +1,10 @@
+import functools
+
 import jax
 import jax.numpy as jnp
 from jax import lax
+from jax.experimental import pallas as pl
+from jax.experimental.pallas import tpu as pltpu
 from jax.sharding import PartitionSpec as P
 
 EPS = 1e-06
@@ -55,6 +59,399 @@
 
 def pass_home(grads):
     return shifted(grads.astype(jnp.bfloat16), "blk", 1).astype(grads.dtype)
+
+
+MESH = pl.DeviceIdType.MESH
+
+
+def where_am_i():
+    place = lax.axis_index("blk")
+    part = lax.axis_index("dp")
+    return {
+        "z": place // 2,
+        "y": lax.rem(place, 2),
+        "x": part // 2,
+        "core": lax.rem(part, 2),
+        "place": place,
+        "part": part,
+    }
+
+
+def peers_of(me):
+    place, part = me["place"], me["part"]
+    return {
+        "core": {"blk": place, "dp": part + 1 - 2 * me["core"]},
+        "x": {"blk": place, "dp": part + 2 - 4 * me["x"]},
+        "y": {"blk": place + 1 - 2 * me["y"], "dp": part},
+        "up": {"blk": place + 2, "dp": part},
+        "down": {"blk": place - 2, "dp": part},
+    }
+
+
+def greet(me, peers, z_count):
+    barrier = pltpu.get_barrier_semaphore()
+    for name in ("core", "x", "y"):
+        pl.semaphore_signal(barrier, inc=1, device_id=peers[name], device_id_type=MESH)
+
+    @pl.when(me["z"] < z_count - 1)
+    def _():
+        pl.semaphore_signal(barrier, inc=1, device_id=peers["up"], device_id_type=MESH)
+
+    @pl.when(me["z"] > 0)
+    def _():
+        pl.semaphore_signal(barrier, inc=1, device_id=peers["down"], device_id_type=MESH)
+
+    ends = (me["z"] == 0).astype(jnp.int32) + (me["z"] == z_count - 1).astype(jnp.int32)
+    pl.semaphore_wait(barrier, 5 - ends)
+
+
+def add_into(target, start, row, extra, count, rows):
+    step = 16
+    for candidate in (160, 128, 80, 64, 48, 32):
+        if rows % candidate == 0:
+            step = candidate
+            break
+
+    def body(index, carry):
+        e = index // (rows // step)
+        at = pl.multiple_of(lax.rem(index, rows // step) * step, 16)
+        here = pl.ds(pl.multiple_of(row + at, 16), step)
+        target[start + e, here, :] = target[start + e, here, :] + extra[e, pl.ds(at, step), :]
+        return carry
+
+    lax.fori_loop(0, count * (rows // step), body, 0)
+
+
+STAGES = 10
+
+
+class Chunk:
+    def __init__(self, number, grad, total, row, rows, first, landing, sems, me, peers, z_count):
+        self.grad, self.total, self.row, self.rows = grad, total, row, rows
+        self.first, self.second = ("x", "y") if first == "x" else ("y", "x")
+        self.land0, self.land1, self.land2 = landing
+        self.send, self.recv, self.local = sems
+        self.number, self.me, self.peers, self.z_count = number, me, peers, z_count
+        self.b1, self.b2, self.core = me[self.first], me[self.second], me["core"]
+        self.quad = 4 * self.core
+        self.pair = self.quad + 2 * self.b1
+        self.own = self.pair + self.b2
+        self.half = rows // 2
+
+    def piece(self, start, count, upper=None):
+        if upper is None:
+            return self.grad.at[pl.ds(start, count), pl.ds(self.row, self.rows), :]
+        row = self.row if upper else self.row + self.half
+        return self.grad.at[pl.ds(start, count), pl.ds(row, self.half), :]
+
+    def spot(self, start, count, upper=None):
+        if upper is None:
+            return self.total.at[pl.ds(start, count), pl.ds(self.row, self.rows), :]
+        row = self.row if upper else self.row + self.half
+        return self.total.at[pl.ds(start, count), pl.ds(row, self.half), :]
+
+    def keep(self, upper):
+        return pltpu.make_async_copy(
+            self.piece(self.own, 1, upper), self.spot(self.own, 1, upper), self.local.at[self.number]
+        )
+
+    def copy(self, stage, peer, source, target):
+        return pltpu.make_async_remote_copy(
+            src_ref=source,
+            dst_ref=target,
+            send_sem=self.send.at[self.number, stage],
+            recv_sem=self.recv.at[self.number, stage],
+            device_id=self.peers[peer],
+            device_id_type=MESH,
+        )
+
+    def reduce_up(self):
+        return self.copy(3, "up", self.piece(self.own, 1, True), self.land2.at[:, pl.ds(self.rows, self.half), :])
+
+    def reduce_down(self):
+        return self.copy(4, "down", self.piece(self.own, 1, False), self.land2.at[:, pl.ds(self.rows + self.half, self.half), :])
+
+    def spread_down(self, fresh=False):
+        here = self.spot(self.own, 1, True)
+        return self.copy(5, "down", self.piece(self.own, 1, True) if fresh else here, here)
+
+    def spread_up(self, fresh=False):
+        here = self.spot(self.own, 1, False)
+        return self.copy(6, "up", self.piece(self.own, 1, False) if fresh else here, here)
+
+    def step0(self):
+        return self.copy(0, "core", self.piece(4 - self.quad, 4), self.land0)
+
+    def step1(self):
+        return self.copy(1, self.first, self.piece(self.quad + 2 - 2 * self.b1, 2), self.land1)
+
+    def step2(self):
+        return self.copy(2, self.second, self.piece(self.pair + 1 - self.b2, 1), self.land2.at[:, pl.ds(0, self.rows), :])
+
+    def gather(self, stage):
+        start, count, peer = ((self.own, 1, self.second), (self.pair, 2, self.first), (self.quad, 4, "core"))[stage - 7]
+        here = self.spot(start, count)
+        return self.copy(stage, peer, here, here)
+
+    def arrive_upper(self):
+        z, last = self.me["z"], self.z_count - 1
+
+        @pl.when(z > 0)
+        def _():
+            self.reduce_up().wait_recv()
+            add_into(self.grad, self.own, self.row, self.land2.at[:, pl.ds(self.rows, self.half), :], 1, self.half)
+
+            @pl.when(z < last)
+            def _():
+                self.reduce_up().start()
+
+            @pl.when(z == last)
+            def _():
+                self.spread_down(True).start()
+                self.keep(True).start()
+
+    def arrive_lower(self):
+        z, last = self.me["z"], self.z_count - 1
+
+        @pl.when(z < last)
+        def _():
+            self.reduce_down().wait_recv()
+            add_into(self.grad, self.own, self.row + self.half, self.land2.at[:, pl.ds(self.rows + self.half, self.half), :], 1, self.half)
+
+            @pl.when(z > 0)
+            def _():
+                self.reduce_down().start()
+
+            @pl.when(z == 0)
+            def _():
+                self.spread_up(True).start()
+                self.keep(False).start()
+
+    def back_upper(self):
+        z, last = self.me["z"], self.z_count - 1
+
+        @pl.when(z < last)
+        def _():
+            self.spread_down().wait_recv()
+
+            @pl.when(z > 0)
+            def _():
+                self.spread_down().start()
+
+    def back_lower(self):
+        z, last = self.me["z"], self.z_count - 1
+
+        @pl.when(z > 0)
+        def _():
+            self.spread_up().wait_recv()
+
+            @pl.when(z < last)
+            def _():
+                self.spread_up().start()
+
+    def tick(self, op):
+        z, last = self.me["z"], self.z_count - 1
+        if op == 0:
+            self.step0().start()
+        elif op == 1:
+            self.step0().wait_recv()
+            add_into(self.grad, self.quad, self.row, self.land0, 4, self.rows)
+            self.step1().start()
+        elif op == 2:
+            self.step1().wait_recv()
+            add_into(self.grad, self.pair, self.row, self.land1, 2, self.rows)
+            self.step2().start()
+        elif op == 3:
+            self.step2().wait_recv()
+            add_into(self.grad, self.own, self.row, self.land2, 1, self.rows)
+
+            @pl.when(z == 0)
+            def _():
+                self.reduce_up().start()
+
+            @pl.when(z == last)
+            def _():
+                self.reduce_down().start()
+
+        elif op == 4:
+            pl.when((z > 0) & (2 * z < self.z_count))(self.arrive_upper)
+            pl.when((z < last) & (2 * z >= self.z_count))(self.arrive_lower)
+        elif op == 5:
+            pl.when((z < last) & (2 * z >= self.z_count))(self.arrive_upper)
+            pl.when((z > 0) & (2 * z < self.z_count))(self.arrive_lower)
+        elif op == 6:
+            pl.when(z == last)(self.arrive_upper)
+            pl.when(z == 0)(self.arrive_lower)
+        elif op == 7:
+            pl.when((z < last) & (2 * z >= self.z_count))(self.back_upper)
+            pl.when((z > 0) & (2 * z < self.z_count))(self.back_lower)
+        elif op == 8:
+
+            @pl.when((z > 0) & (2 * z < self.z_count))
+            def _():
+                self.back_upper()
+                self.gather(7).start()
+
+            @pl.when((z < last) & (2 * z >= self.z_count))
+            def _():
+                self.back_lower()
+                self.gather(7).start()
+
+        elif op == 9:
+
+            @pl.when(z == 0)
+            def _():
+                self.back_upper()
+                self.keep(False).wait()
+                self.gather(7).start()
+
+            @pl.when(z == last)
+            def _():
+                self.back_lower()
+                self.keep(True).wait()
+                self.gather(7).start()
+
+        elif op == 10:
+            self.gather(7).wait_recv()
+            self.gather(8).start()
+        elif op == 11:
+            self.gather(8).wait_recv()
+            self.gather(9).start()
+        elif op == 12:
+            self.gather(9).wait_recv()
+            self.drain()
+
+    OPS = 13
+
+    def drain(self):
+        z, last = self.me["z"], self.z_count - 1
+        self.step0().wait_send()
+        self.step1().wait_send()
+        self.step2().wait_send()
+        for stage in (7, 8, 9):
+            self.gather(stage).wait_send()
+
+        @pl.when(z < last)
+        def _():
+            self.reduce_up().wait_send()
+            self.spread_up().wait_send()
+
+        @pl.when(z > 0)
+        def _():
+            self.reduce_down().wait_send()
+            self.spread_down().wait_send()
+
+
+def sum_kernel(z_count, plan, *refs):
+    n = 1 + max(item[0] for item in plan)
+    parts = len(plan)
+    ins, outs = refs[:n], refs[n : 2 * n]
+    rest = refs[2 * n :]
+    grads, rest = rest[:n], rest[n:]
+    landings = rest[: 3 * parts]
+    send, recv, local, load = rest[3 * parts :]
+    me = where_am_i()
+    peers = peers_of(me)
+    loads = [pltpu.make_async_copy(ins[i], grads[i], load.at[i]) for i in range(n)]
+    for item in loads:
+        item.start()
+    greet(me, peers, z_count)
+    for item in loads:
+        item.wait()
+    chunks = []
+    for number, (i, row, rows, first) in enumerate(plan):
+        landing = landings[3 * number : 3 * number + 3]
+        chunks.append(
+            Chunk(number, grads[i], outs[i], row, rows, first, landing, (send, recv, local), me, peers, z_count)
+        )
+    for at in range(parts + Chunk.OPS - 1):
+        for number in range(parts):
+            if 0 <= at - number < Chunk.OPS:
+                chunks[number].tick(at - number)
+
+
+def sum_call(arrays, plan, z_count):
+    landing = []
+    for i, row, rows, first in plan:
+        columns, kind = arrays[i].shape[2], arrays[i].dtype
+        landing += [
+            pltpu.VMEM((4, rows, columns), kind),
+            pltpu.VMEM((2, rows, columns), kind),
+            pltpu.VMEM((1, 2 * rows, columns), kind),
+        ]
+    n = len(arrays)
+    return pl.pallas_call(
+        functools.partial(sum_kernel, z_count, plan),
+        out_shape=tuple(jax.ShapeDtypeStruct(v.shape, v.dtype) for v in arrays),
+        in_specs=[pl.BlockSpec(memory_space=pl.ANY)] * n,
+        out_specs=tuple([pl.BlockSpec(memory_space=pl.ANY)] * n),
+        scratch_shapes=[pltpu.VMEM(v.shape, v.dtype) for v in arrays]
+        + landing
+        + [
+            pltpu.SemaphoreType.DMA((len(plan), STAGES)),
+            pltpu.SemaphoreType.DMA((len(plan), STAGES)),
+            pltpu.SemaphoreType.DMA((len(plan),)),
+            pltpu.SemaphoreType.DMA((n,)),
+        ],
+        compiler_params=pltpu.CompilerParams(
+            collective_id=0, has_side_effects=True, vmem_limit_bytes=56 * 2**20
+        ),
+    )(*arrays)
+
+
+def columns_to_panels(value):
+    rows, columns = value.shape
+    return jnp.transpose(value.reshape(rows, 8, columns // 8), (1, 0, 2)).astype(jnp.bfloat16)
+
+
+def panels_to_columns(panels):
+    count, rows, width = panels.shape
+    return jnp.transpose(panels.astype(jnp.float32), (1, 0, 2)).reshape(rows, count * width)
+
+
+def sum_gradients(grads):
+    (g_in, g_query, g_key, g_value, g_qgain, g_kgain, g_out, g_attn, g_pre, g_gate, g_up, g_down, g_post) = grads
+    z_count = lax.axis_size("blk") // 2
+    width = g_in.shape[0]
+    gains = [g_in, g_attn, g_pre, g_post, g_qgain, g_kgain]
+    sizes = [v.shape[0] for v in gains]
+    flat = jnp.concatenate(gains)
+    gain_rows = 32
+    flat = jnp.pad(flat, (0, 8 * gain_rows * 128 - flat.shape[0])).reshape(8, gain_rows, 128)
+    down = g_down.astype(jnp.bfloat16).reshape(8, -1, width)
+    out = g_out.astype(jnp.bfloat16).reshape(8, -1, width)
+    both = jnp.stack([g_key, g_value])
+    head = g_key.shape[1]
+    both = jnp.transpose(both.reshape(2, 2, width // 2, 2, head // 2), (0, 1, 3, 2, 4)).reshape(8, width // 2, head // 2)
+    arrays = [down, columns_to_panels(g_gate), columns_to_panels(g_up), out, columns_to_panels(g_query), both.astype(jnp.bfloat16), flat]
+    plan = []
+    for i, v in enumerate(arrays[:-1]):
+        rows = v.shape[1] // 2
+        plan += [(i, 0, rows, "x"), (i, rows, rows, "y")]
+    plan.append((6, 0, gain_rows, "x"))
+    down, gate, up, out, query, both, flat = sum_call(arrays, plan, z_count)
+    both = jnp.transpose(both.astype(jnp.float32).reshape(2, 2, 2, width // 2, head // 2), (0, 1, 3, 2, 4)).reshape(2, width, head)
+    flat = flat.reshape(-1)
+    cuts, at = [], 0
+    for size in sizes:
+        cuts.append(flat[at : at + size])
+        at += size
+    g_in, g_attn, g_pre, g_post, g_qgain, g_kgain = cuts
+    return (
+        g_in,
+        panels_to_columns(query),
+        both[0],
+        both[1],
+        g_qgain,
+        g_kgain,
+        out.astype(jnp.float32).reshape(g_out.shape),
+        g_attn,
+        g_pre,
+        panels_to_columns(gate),
+        panels_to_columns(up),
+        down.astype(jnp.float32).reshape(g_down.shape),
+        g_post,
+    )
 
 
 def per_device(
@@ -237,7 +634,7 @@
         g_up,
         g_down,
         g_post,
-    ) = lax.psum(
+    ) = sum_gradients(
         (
             g_in,
             g_query,
@@ -252,8 +649,7 @@
             g_up,
             g_down,
             g_post,
-        ),
-        ("blk", "dp"),
+        )
     )
     return (
         output.astype(jnp.bfloat16)[None],

time: 791 us -> 631 us (0.80)
  waiting for transfers between devices: 417 us -> 70 us
  Pallas kernels: 0 us -> 185 us
  blocking collectives: 43.7 us -> 0 us
  local copies, waits for them, and re-layouts: 69.2 us -> 106 us
  other arithmetic: 36.3 us -> 51 us
  between operations: 15.4 us -> 1.85 us
  starting transfers between devices: 93.6 us -> 104 us
    psum x1 -> x0, waiting for transfers between devices: 324 us -> none  [per_device(): lax.psum((g_in, g_query, g_key, g_value, g_qgain, g_kgain, g_out, g_attn,...]
    pallas_call x0 -> x1, Pallas kernels: none -> 185 us  [sum_call(): pl.pallas_call(functools.partial(sum_kernel, z_count, plan), out_shape=tu...]
    psum x1 -> x0, blocking collectives: 43.7 us -> none  [per_device(): lax.psum((g_in, g_query, g_key, g_value, g_qgain, g_kgain, g_out, g_attn,...]
    ppermute x14, waiting for transfers between devices: 93.3 us -> 53.4 us  [from_behind(): return lax.ppermute(block, axis, route)]
    convert_element_type x0 -> x4, local copies, waits for them, and re-layouts: none -> 17.6 us  [columns_to_panels(): jnp.transpose(value.reshape(rows, 8, columns // 8), (1, 0, 2))]
    ppermute x8, waiting for transfers between devices: 0.02 us -> 16.6 us  [shifted(): lax.ppermute(array, axis, [(i, (i + by) % peers) for i in range(peers)])]
    reshape x0 -> x3, local copies, waits for them, and re-layouts: none -> 14.1 us  [panels_to_columns(): jnp.transpose(panels.astype(jnp.float32), (1, 0, 2))]
    reshape x0 -> x4, other arithmetic: none -> 12.6 us  [the longest x2 7.92 us: panels_to_columns(): jnp.transpose(panels.astype(jnp.float32), (1, 0, 2))]
  transfers between devices with their start and end apart: 23 -> 22, of which waited for: 15 -> 21; matrix products, arithmetic and copies ran while one was open for 8% -> 12% of each run, Pallas kernels for 0% -> 0%
where the time goes in v1:
time: 631 us; the launch traced here: 622 us
  Pallas kernels  185 us (29%)
  local copies, waits for them, and re-layouts  106 us (17%)
  starting transfers between devices  104 us (16%)
  matrix products  103 us (16%)
  waiting for transfers between devices  70 us (11%)
  other arithmetic  51 us (8%)
    pallas_call x1, Pallas kernels, sum_call(): pl.pallas_call(functools.partial(sum_kernel, z_count, plan), out_shape=tu...  185 us
    ppermute x14, starting transfers between devices, from_behind(): return lax.ppermute(block, axis, route)  77.8 us
    ppermute x14, waiting for transfers between devices, from_behind(): return lax.ppermute(block, axis, route)  53.4 us
    unnamed x168, local copies, waits for them, and re-layouts  29 us
    ppermute x8, starting transfers between devices, shifted(): lax.ppermute(array, axis, [(i, (i + by) % peers) for i in range(peers)])  26.7 us
    while x63, local copies, waits for them, and re-layouts  25.7 us
    dot_general x8, matrix products, absorb(): jnp.einsum('hqk,kd->hqd', expo.astype(jnp.bfloat16), pair[1], preferred_e...  19.6 us
    convert_element_type x4, local copies, waits for them, and re-layouts, columns_to_panels(): jnp.transpose(value.reshape(rows, 8, columns // 8), (1, 0, 2))  17.6 us
  transfers between devices with their start and end apart: 22, of which 21 were waited for; matrix products, arithmetic and copies ran while one was open for 12% of the time, Pallas kernels for 0%

profile of v1, /device:TPU:0, one launch (start us, length us, event | category | flops | bytes accessed | tf_op | source)
XLA Modules:
  0.0 622.2 jit_solution(5317424430264456250)
XLA Ops:
  29.0 132.1 %while.42 = (s32[]{:T(128)}, f32[4,384,1]{1,0,2:T(4,128)S(1)}, f32[4,384,1]{1,0,2:T(4,128)S(1)}, f32[4,384,256]{2,1,0:T(8,128)}, bf16[2,384,256]{2,1,0:T(8,128)(...) while((s32[]{:T(128)}, f32[4,384,1]{1,0,2:T(4,128)S(1)}, ...), condition=%wide.region_13.14_spmd.clone, body=%wide.region_9.13_spmd.clone.sunk | while | flops 612885888 | bytes 27046280 | solution.py:530
  29.0 5.6 collective-permute-start
  34.9 7.6 %collective-permute-done = bf16[2,384,256]{2,1,0:T(8,128)(2,1)} collective-permute-done((bf16[2,384,256]{2,1,0:T(8,128)(2,1)}, bf16[2,384,256]{2,1,0:T(8,128)(2,1)}, u32[]{:S(2)}, u32[]{:S(2)}) %collective-permute-start) | collective-permute-done | bytes 393248 | tf_op jit(solution)/shard_map/while/body/eval_jaxpr/ppermute | solution.py:23
  49.8 5.1 collective-permute-start
  55.3 6.8 %collective-permute-done = bf16[2,384,256]{2,1,0:T(8,128)(2,1)} collective-permute-done((bf16[2,384,256]{2,1,0:T(8,128)(2,1)}, bf16[2,384,256]{2,1,0:T(8,128)(2,1)}, u32[]{:S(2)}, u32[]{:S(2)}) %collective-permute-start) | collective-permute-done | bytes 393248 | tf_op jit(solution)/shard_map/while/body/eval_jaxpr/ppermute | solution.py:23
  69.3 5.1 collective-permute-start
  74.8 5.8 collective-permute-done
  87.9 5.9 collective-permute-start
  106.3 6.0 collective-permute-start
  124.5 6.0 collective-permute-start
  142.7 6.0 collective-permute-start
  198.8 133.4 %while.43 = (s32[]{:T(128)}, f32[4,384,256]{2,1,0:T(8,128)S(1)}, bf16[2,384,256]{2,1,0:T(8,128)(2,1)}, bf16[2,384,256]{2,1,0:T(8,128)(2,1)}, s32[384]{0:T(512)S(...) while((s32[]{:T(128)}, f32[4,384,256]{2,1,0:T(8,128)S(1)}, ...), condition=%wide.region_23.24_spmd.clone, body=%wide.region_21.23_spmd.clone.sunk | while | flops 1518064512 | bytes 27408804 | solution.py:595
  198.8 5.3 collective-permute-start.1
  234.3 5.5 collective-permute-start.1
  252.8 5.5 collective-permute-start.1
  271.9 5.5 collective-permute-start.1
  291.6 5.5 collective-permute-start.1
  311.8 5.5 collective-permute-start.1
  389.1 184.9 %shard_map.271 = (bf16[8,256,640]{2,1,0:T(8,128)(2,1)}, bf16[8,640,256]{2,1,0:T(8,128)(2,1)}, bf16[8,640,256]{2,1,0:T(8,128)(2,1)}, bf16[8,128,640]{2,1,0:T(8,12...) custom-call(bf16[8,256,640]{2,1,0:T(8,128)(2,1)} %bitcast.343, ...), custom_call_target="tpu_custom_call" | custom-call | tf_op jit(solution)/shard_map/pallas_call | solution.py:383
  576.7 7.7 %convert_bitcast_fusion = (f32[640,8,256]{2,0,1:T(8,128)}, f32[640,8,256]{2,0,1:T(8,128)}) fusion(bf16[8,640,256]{2,1,0:T(8,128)(2,1)} %get-tuple-element.569, bf16[8,640,256]{2,1,0:T(8,128)(2,1)} %get-tuple-element.568), kind=kLoop, calls=%fused_computation.47 | loop fusion | flops 2621440 | bytes 15728640 | tf_op jit(solution)/shard_map/reshape | solution.py:409
  584.4 6.1 copy.132
  590.6 5.9 copy.135
  596.4 5.9 copy.133
  602.4 5.9 copy.136
  (488 shorter events, 309.8 us)
Async XLA Ops:
  0.6 169.4 %copy-start = (bf16[640,2048]{1,0:T(8,128)(2,1)S(1)}, bf16[640,2048]{1,0:T(8,128)(2,1)}, u32[]{:S(2)}) copy-start(bf16[640,2048]{1,0:T(8,128)(2,1)} %param.33) | copy-start | bytes 7864324
  0.7 12.7 %copy-start.73 = (f32[128]{0:T(128)}, f32[128]{0:T(128)S(1)}, u32[]{:S(2)}) copy-start(f32[128]{0:T(128)S(1)} %multiply_exponential_fusion) | copy-start | bytes 1540
  29.0 13.5 %collective-permute-start = (bf16[2,384,256]{2,1,0:T(8,128)(2,1)}, bf16[2,384,256]{2,1,0:T(8,128)(2,1)}, u32[]{:S(2)}, u32[]{:S(2)}) collective-permute-start(bf16[2,384,256]{2,1,0:T(8,128)(2,1)} %get-tuple-element.994), channel_id=1, source_target_pairs={{0,4},{4,8},{8,12},{12,16},{16,20},{20,24},{24,28},{1,5},{5,9},{9,... | collective-permute-start | bytes 1179656 | tf_op jit(solution)/shard_map/while/body/eval_jaxpr/ppermute | solution.py:23
  49.8 12.2 %collective-permute-start = (bf16[2,384,256]{2,1,0:T(8,128)(2,1)}, bf16[2,384,256]{2,1,0:T(8,128)(2,1)}, u32[]{:S(2)}, u32[]{:S(2)}) collective-permute-start(bf16[2,384,256]{2,1,0:T(8,128)(2,1)} %get-tuple-element.994), channel_id=1, source_target_pairs={{0,4},{4,8},{8,12},{12,16},{16,20},{20,24},{24,28},{1,5},{5,9},{9,... | collective-permute-start | bytes 1179656 | tf_op jit(solution)/shard_map/while/body/eval_jaxpr/ppermute | solution.py:23
  69.3 11.3 %collective-permute-start = (bf16[2,384,256]{2,1,0:T(8,128)(2,1)}, bf16[2,384,256]{2,1,0:T(8,128)(2,1)}, u32[]{:S(2)}, u32[]{:S(2)}) collective-permute-start(bf16[2,384,256]{2,1,0:T(8,128)(2,1)} %get-tuple-element.994), channel_id=1, source_target_pairs={{0,4},{4,8},{8,12},{12,16},{16,20},{20,24},{24,28},{1,5},{5,9},{9,... | collective-permute-start | bytes 1179656 | tf_op jit(solution)/shard_map/while/body/eval_jaxpr/ppermute | solution.py:23
  87.9 11.1 %collective-permute-start = (bf16[2,384,256]{2,1,0:T(8,128)(2,1)}, bf16[2,384,256]{2,1,0:T(8,128)(2,1)}, u32[]{:S(2)}, u32[]{:S(2)}) collective-permute-start(bf16[2,384,256]{2,1,0:T(8,128)(2,1)} %get-tuple-element.994), channel_id=1, source_target_pairs={{0,4},{4,8},{8,12},{12,16},{16,20},{20,24},{24,28},{1,5},{5,9},{9,... | collective-permute-start | bytes 1179656 | tf_op jit(solution)/shard_map/while/body/eval_jaxpr/ppermute | solution.py:23
  106.3 10.9 %collective-permute-start = (bf16[2,384,256]{2,1,0:T(8,128)(2,1)}, bf16[2,384,256]{2,1,0:T(8,128)(2,1)}, u32[]{:S(2)}, u32[]{:S(2)}) collective-permute-start(bf16[2,384,256]{2,1,0:T(8,128)(2,1)} %get-tuple-element.994), channel_id=1, source_target_pairs={{0,4},{4,8},{8,12},{12,16},{16,20},{20,24},{24,28},{1,5},{5,9},{9,... | collective-permute-start | bytes 1179656 | tf_op jit(solution)/shard_map/while/body/eval_jaxpr/ppermute | solution.py:23
  124.5 10.9 %collective-permute-start = (bf16[2,384,256]{2,1,0:T(8,128)(2,1)}, bf16[2,384,256]{2,1,0:T(8,128)(2,1)}, u32[]{:S(2)}, u32[]{:S(2)}) collective-permute-start(bf16[2,384,256]{2,1,0:T(8,128)(2,1)} %get-tuple-element.994), channel_id=1, source_target_pairs={{0,4},{4,8},{8,12},{12,16},{16,20},{20,24},{24,28},{1,5},{5,9},{9,... | collective-permute-start | bytes 1179656 | tf_op jit(solution)/shard_map/while/body/eval_jaxpr/ppermute | solution.py:23
  142.7 10.9 %collective-permute-start = (bf16[2,384,256]{2,1,0:T(8,128)(2,1)}, bf16[2,384,256]{2,1,0:T(8,128)(2,1)}, u32[]{:S(2)}, u32[]{:S(2)}) collective-permute-start(bf16[2,384,256]{2,1,0:T(8,128)(2,1)} %get-tuple-element.994), channel_id=1, source_target_pairs={{0,4},{4,8},{8,12},{12,16},{16,20},{20,24},{24,28},{1,5},{5,9},{9,... | collective-permute-start | bytes 1179656 | tf_op jit(solution)/shard_map/while/body/eval_jaxpr/ppermute | solution.py:23
  198.8 11.4 %collective-permute-start.1 = (bf16[2,384,256]{2,1,0:T(8,128)(2,1)}, bf16[2,384,256]{2,1,0:T(8,128)(2,1)S(1)}, u32[]{:S(2)}, u32[]{:S(2)}) collective-permute-start(bf16[2,384,256]{2,1,0:T(8,128)(2,1)} %get-tuple-element.1039), channel_id=1, source_target_pairs={{0,4},{4,8},{8,12},{12,16},{16,20},{20,24},{24,28},{1,5},{5,9},{9,... | collective-permute-start | bytes 1179656 | tf_op jit(solution)/shard_map/while/body/eval_jaxpr/ppermute | solution.py:23
  204.1 11.7 %collective-permute-start.2 = (bf16[2,384,256]{2,1,0:T(8,128)(2,1)}, bf16[2,384,256]{2,1,0:T(8,128)(2,1)S(1)}, u32[]{:S(2)}, u32[]{:S(2)}) collective-permute-start(bf16[2,384,256]{2,1,0:T(8,128)(2,1)} %get-tuple-element.1040), channel_id=1, source_target_pairs={{0,4},{4,8},{8,12},{12,16},{16,20},{20,24},{24,28},{28,0},{1,5},{5... | collective-permute-start | bytes 1179656 | tf_op jit(solution)/shard_map/while/body/eval_jaxpr/ppermute | solution.py:17
  216.7 10.7 %collective-permute-start.1 = (bf16[2,384,256]{2,1,0:T(8,128)(2,1)}, bf16[2,384,256]{2,1,0:T(8,128)(2,1)S(1)}, u32[]{:S(2)}, u32[]{:S(2)}) collective-permute-start(bf16[2,384,256]{2,1,0:T(8,128)(2,1)} %get-tuple-element.1039), channel_id=1, source_target_pairs={{0,4},{4,8},{8,12},{12,16},{16,20},{20,24},{24,28},{1,5},{5,9},{9,... | collective-permute-start | bytes 1179656 | tf_op jit(solution)/shard_map/while/body/eval_jaxpr/ppermute | solution.py:23
  221.8 11.6 %collective-permute-start.2 = (bf16[2,384,256]{2,1,0:T(8,128)(2,1)}, bf16[2,384,256]{2,1,0:T(8,128)(2,1)S(1)}, u32[]{:S(2)}, u32[]{:S(2)}) collective-permute-start(bf16[2,384,256]{2,1,0:T(8,128)(2,1)} %get-tuple-element.1040), channel_id=1, source_target_pairs={{0,4},{4,8},{8,12},{12,16},{16,20},{20,24},{24,28},{28,0},{1,5},{5... | collective-permute-start | bytes 1179656 | tf_op jit(solution)/shard_map/while/body/eval_jaxpr/ppermute | solution.py:17
  234.3 11.0 %collective-permute-start.1 = (bf16[2,384,256]{2,1,0:T(8,128)(2,1)}, bf16[2,384,256]{2,1,0:T(8,128)(2,1)S(1)}, u32[]{:S(2)}, u32[]{:S(2)}) collective-permute-start(bf16[2,384,256]{2,1,0:T(8,128)(2,1)} %get-tuple-element.1039), channel_id=1, source_target_pairs={{0,4},{4,8},{8,12},{12,16},{16,20},{20,24},{24,28},{1,5},{5,9},{9,... | collective-permute-start | bytes 1179656 | tf_op jit(solution)/shard_map/while/body/eval_jaxpr/ppermute | solution.py:23
  239.8 12.2 %collective-permute-start.2 = (bf16[2,384,256]{2,1,0:T(8,128)(2,1)}, bf16[2,384,256]{2,1,0:T(8,128)(2,1)S(1)}, u32[]{:S(2)}, u32[]{:S(2)}) collective-permute-start(bf16[2,384,256]{2,1,0:T(8,128)(2,1)} %get-tuple-element.1040), channel_id=1, source_target_pairs={{0,4},{4,8},{8,12},{12,16},{16,20},{20,24},{24,28},{28,0},{1,5},{5... | collective-permute-start | bytes 1179656 | tf_op jit(solution)/shard_map/while/body/eval_jaxpr/ppermute | solution.py:17
  252.8 11.1 %collective-permute-start.1 = (bf16[2,384,256]{2,1,0:T(8,128)(2,1)}, bf16[2,384,256]{2,1,0:T(8,128)(2,1)S(1)}, u32[]{:S(2)}, u32[]{:S(2)}) collective-permute-start(bf16[2,384,256]{2,1,0:T(8,128)(2,1)} %get-tuple-element.1039), channel_id=1, source_target_pairs={{0,4},{4,8},{8,12},{12,16},{16,20},{20,24},{24,28},{1,5},{5,9},{9,... | collective-permute-start | bytes 1179656 | tf_op jit(solution)/shard_map/while/body/eval_jaxpr/ppermute | solution.py:23
  258.3 12.8 %collective-permute-start.2 = (bf16[2,384,256]{2,1,0:T(8,128)(2,1)}, bf16[2,384,256]{2,1,0:T(8,128)(2,1)S(1)}, u32[]{:S(2)}, u32[]{:S(2)}) collective-permute-start(bf16[2,384,256]{2,1,0:T(8,128)(2,1)} %get-tuple-element.1040), channel_id=1, source_target_pairs={{0,4},{4,8},{8,12},{12,16},{16,20},{20,24},{24,28},{28,0},{1,5},{5... | collective-permute-start | bytes 1179656 | tf_op jit(solution)/shard_map/while/body/eval_jaxpr/ppermute | solution.py:17
  271.9 11.1 %collective-permute-start.1 = (bf16[2,384,256]{2,1,0:T(8,128)(2,1)}, bf16[2,384,256]{2,1,0:T(8,128)(2,1)S(1)}, u32[]{:S(2)}, u32[]{:S(2)}) collective-permute-start(bf16[2,384,256]{2,1,0:T(8,128)(2,1)} %get-tuple-element.1039), channel_id=1, source_target_pairs={{0,4},{4,8},{8,12},{12,16},{16,20},{20,24},{24,28},{1,5},{5,9},{9,... | collective-permute-start | bytes 1179656 | tf_op jit(solution)/shard_map/while/body/eval_jaxpr/ppermute | solution.py:23
  277.4 13.3 %collective-permute-start.2 = (bf16[2,384,256]{2,1,0:T(8,128)(2,1)}, bf16[2,384,256]{2,1,0:T(8,128)(2,1)S(1)}, u32[]{:S(2)}, u32[]{:S(2)}) collective-permute-start(bf16[2,384,256]{2,1,0:T(8,128)(2,1)} %get-tuple-element.1040), channel_id=1, source_target_pairs={{0,4},{4,8},{8,12},{12,16},{16,20},{20,24},{24,28},{28,0},{1,5},{5... | collective-permute-start | bytes 1179656 | tf_op jit(solution)/shard_map/while/body/eval_jaxpr/ppermute | solution.py:17
  291.6 11.1 %collective-permute-start.1 = (bf16[2,384,256]{2,1,0:T(8,128)(2,1)}, bf16[2,384,256]{2,1,0:T(8,128)(2,1)S(1)}, u32[]{:S(2)}, u32[]{:S(2)}) collective-permute-start(bf16[2,384,256]{2,1,0:T(8,128)(2,1)} %get-tuple-element.1039), channel_id=1, source_target_pairs={{0,4},{4,8},{8,12},{12,16},{16,20},{20,24},{24,28},{1,5},{5,9},{9,... | collective-permute-start | bytes 1179656 | tf_op jit(solution)/shard_map/while/body/eval_jaxpr/ppermute | solution.py:23
  297.1 13.9 %collective-permute-start.2 = (bf16[2,384,256]{2,1,0:T(8,128)(2,1)}, bf16[2,384,256]{2,1,0:T(8,128)(2,1)S(1)}, u32[]{:S(2)}, u32[]{:S(2)}) collective-permute-start(bf16[2,384,256]{2,1,0:T(8,128)(2,1)} %get-tuple-element.1040), channel_id=1, source_target_pairs={{0,4},{4,8},{8,12},{12,16},{16,20},{20,24},{24,28},{28,0},{1,5},{5... | collective-permute-start | bytes 1179656 | tf_op jit(solution)/shard_map/while/body/eval_jaxpr/ppermute | solution.py:17
  311.8 11.5 %collective-permute-start.1 = (bf16[2,384,256]{2,1,0:T(8,128)(2,1)}, bf16[2,384,256]{2,1,0:T(8,128)(2,1)S(1)}, u32[]{:S(2)}, u32[]{:S(2)}) collective-permute-start(bf16[2,384,256]{2,1,0:T(8,128)(2,1)} %get-tuple-element.1039), channel_id=1, source_target_pairs={{0,4},{4,8},{8,12},{12,16},{16,20},{20,24},{24,28},{1,5},{5,9},{9,... | collective-permute-start | bytes 1179656 | tf_op jit(solution)/shard_map/while/body/eval_jaxpr/ppermute | solution.py:23
  317.3 14.0 %collective-permute-start.2 = (bf16[2,384,256]{2,1,0:T(8,128)(2,1)}, bf16[2,384,256]{2,1,0:T(8,128)(2,1)S(1)}, u32[]{:S(2)}, u32[]{:S(2)}) collective-permute-start(bf16[2,384,256]{2,1,0:T(8,128)(2,1)} %get-tuple-element.1040), channel_id=1, source_target_pairs={{0,4},{4,8},{8,12},{12,16},{16,20},{20,24},{24,28},{28,0},{1,5},{5... | collective-permute-start | bytes 1179656 | tf_op jit(solution)/shard_map/while/body/eval_jaxpr/ppermute | solution.py:17
  334.1 43.3 %collective-permute-start.3 = (bf16[2,384,256]{1,2,0:T(8,128)(2,1)}, bf16[2,384,256]{1,2,0:T(8,128)(2,1)}, u32[]{:S(2)}, u32[]{:S(2)}) collective-permute-start(bf16[2,384,256]{1,2,0:T(8,128)(2,1)} %copy.121), channel_id=1, source_target_pairs={{0,4},{4,8},{8,12},{12,16},{16,20},{20,24},{24,28},{28,0},{1,5},{5... | collective-permute-start | bytes 1179656 | tf_op jit(solution)/shard_map/ppermute | solution.py:17
  (97 other events, 239.1 us)

commit v2 on v1

--- a/solution.py
+++ b/solution.py
@@ -106,7 +106,7 @@
 
 
 def add_into(target, start, row, extra, count, rows):
-    step = 16
+    step = rows if rows < 32 else 16
     for candidate in (160, 128, 80, 64, 48, 32):
         if rows % candidate == 0:
             step = candidate
@@ -114,8 +114,8 @@
 
     def body(index, carry):
         e = index // (rows // step)
-        at = pl.multiple_of(lax.rem(index, rows // step) * step, 16)
-        here = pl.ds(pl.multiple_of(row + at, 16), step)
+        at = pl.multiple_of(lax.rem(index, rows // step) * step, 8)
+        here = pl.ds(pl.multiple_of(row + at, 8), step)
         target[start + e, here, :] = target[start + e, here, :] + extra[e, pl.ds(at, step), :]
         return carry
 
@@ -144,15 +144,30 @@
         row = self.row if upper else self.row + self.half
         return self.grad.at[pl.ds(start, count), pl.ds(row, self.half), :]
 
-    def spot(self, start, count, upper=None):
-        if upper is None:
-            return self.total.at[pl.ds(start, count), pl.ds(self.row, self.rows), :]
-        row = self.row if upper else self.row + self.half
-        return self.total.at[pl.ds(start, count), pl.ds(row, self.half), :]
+    def spot(self, count, upper=None):
+        row, rows = self.row, self.rows
+        if upper is not None:
+            row, rows = (row if upper else row + self.half), self.half
+        here, columns = pl.ds(row, rows), self.grad.shape[2]
+        start = {1: self.own, 2: self.pair, 4: self.quad}[count]
+        if len(self.total.shape) == 2:
+            return self.total.at[here, pl.ds(pl.multiple_of(start * columns, 128), count * columns)]
+        if len(self.total.shape) == 4:
+            if count == 4:
+                return self.total.at[self.core, :, here, :]
+            if count == 2:
+                return self.total.at[self.core, self.b1, here, :]
+            return self.total.at[self.core, self.b1, here, pl.ds(pl.multiple_of(self.b2 * columns, 128), columns)]
+        if count == 1:
+            return self.total.at[start, here, :]
+        return self.total.at[pl.ds(start, count), here, :]
+
+    def mine(self, upper):
+        return self.grad.at[self.own, pl.ds(self.row if upper else self.row + self.half, self.half), :]
 
     def keep(self, upper):
         return pltpu.make_async_copy(
-            self.piece(self.own, 1, upper), self.spot(self.own, 1, upper), self.local.at[self.number]
+            self.mine(upper), self.spot(1, upper), self.local.at[self.number]
         )
 
     def copy(self, stage, peer, source, target):
@@ -172,12 +187,12 @@
         return self.copy(4, "down", self.piece(self.own, 1, False), self.land2.at[:, pl.ds(self.rows + self.half, self.half), :])
 
     def spread_down(self, fresh=False):
-        here = self.spot(self.own, 1, True)
-        return self.copy(5, "down", self.piece(self.own, 1, True) if fresh else here, here)
+        here = self.spot(1, True)
+        return self.copy(5, "down", self.mine(True) if fresh else here, here)
 
     def spread_up(self, fresh=False):
-        here = self.spot(self.own, 1, False)
-        return self.copy(6, "up", self.piece(self.own, 1, False) if fresh else here, here)
+        here = self.spot(1, False)
+        return self.copy(6, "up", self.mine(False) if fresh else here, here)
 
     def step0(self):
         return self.copy(0, "core", self.piece(4 - self.quad, 4), self.land0)
@@ -189,8 +204,8 @@
         return self.copy(2, self.second, self.piece(self.pair + 1 - self.b2, 1), self.land2.at[:, pl.ds(0, self.rows), :])
 
     def gather(self, stage):
-        start, count, peer = ((self.own, 1, self.second), (self.pair, 2, self.first), (self.quad, 4, "core"))[stage - 7]
-        here = self.spot(start, count)
+        count, peer = ((1, self.second), (2, self.first), (4, "core"))[stage - 7]
+        here = self.spot(count)
         return self.copy(stage, peer, here, here)
 
     def arrive_upper(self):
@@ -454,6 +469,619 @@
     )
 
 
+LOG2E = 1.4426950408889634
+LN2 = 0.6931471805599453
+
+
+def dot(left, right):
+    return jnp.dot(left, right, preferred_element_type=jnp.float32)
+
+
+def dot_nt(left, right):
+    return lax.dot_general(left, right, (((1,), (1,)), ((), ())), preferred_element_type=jnp.float32)
+
+
+def inverse_rms(value):
+    return lax.rsqrt(jnp.mean(value * value, axis=-1, keepdims=True) + EPS)
+
+
+def rms_back(value, inverse, gain, grad):
+    scaled = grad * gain
+    normal = value * inverse
+    mean = jnp.mean(scaled * normal, axis=-1, keepdims=True)
+    terms = grad * normal
+    return inverse * (scaled - normal * mean), jnp.sum(terms.reshape(-1, 8, terms.shape[-1]), axis=0)
+
+
+def turn(value, cosine, sine):
+    half = value.shape[-1] // 2
+    first, second = value[:, :half], value[:, half:]
+    return jnp.concatenate([first * cosine - second * sine, second * cosine + first * sine], axis=-1)
+
+
+def turn_back(grad, cosine, sine):
+    half = grad.shape[-1] // 2
+    first, second = grad[:, :half], grad[:, half:]
+    return jnp.concatenate([first * cosine + second * sine, second * cosine - first * sine], axis=-1)
+
+
+def bf16(value):
+    return value.astype(jnp.bfloat16)
+
+
+def f32(value):
+    return value.astype(jnp.float32)
+
+
+class Reducer:
+    def __init__(self):
+        self.waiting, self.active = [], []
+
+    def add(self, *chunks):
+        self.waiting += chunks
+
+    def tick(self):
+        self.active = [item for item in self.active if item[1] < Chunk.OPS]
+        if self.waiting:
+            self.active.append([self.waiting.pop(0), 0])
+        for item in self.active:
+            item[0].tick(item[1])
+            item[1] += 1
+        return bool(self.active)
+
+    def finish(self):
+        while self.tick():
+            pass
+
+
+class Names(dict):
+    __getattr__ = dict.__getitem__
+
+
+def layer_kernel(sizes, names, *refs):
+    r = Names(zip(names, refs, strict=True))
+    rows, width, hidden, heads, head, z_count = sizes
+    scale = head**-0.5
+    tile = 128
+    tiles = [slice(at, at + tile) for at in range(0, rows, tile)]
+    half = head // 2
+    me = where_am_i()
+    peers = peers_of(me)
+    z, y, place = me["z"], me["y"], me["place"]
+    last = z_count - 1
+
+    weights = ["x", "w_key", "w_value", "w_query", "w_out", "w_gate", "w_up", "w_down", "dy"]
+    joined = heads * head
+    wide_k, wide_v = slice(joined, joined + head), slice(joined + head, joined + 2 * head)
+    spots = {"w_query": slice(0, joined), "w_key": wide_k, "w_value": wide_v}
+    loads = {}
+    for i, name in enumerate(weights):
+        spot = r.w_first.at[:, spots[name]] if name in spots else r[name]
+        loads[name] = pltpu.make_async_copy(r[name + "_in"], spot, r.load_sem.at[i])
+    for name in weights:
+        loads[name].start()
+    greet(me, peers, z_count)
+
+    token = place * rows + lax.broadcasted_iota(jnp.int32, (1, rows), 1)
+    begin = jnp.zeros((1, rows), jnp.int32)
+    end = jnp.int32(0)
+    for j in range(r.lengths.shape[1]):
+        end = end + r.lengths[0, j]
+        begin = jnp.where(token >= end, end, begin)
+
+    def allowed(source, at, count):
+        key = source * rows + at + lax.broadcasted_iota(jnp.int32, (count, rows), 0)
+        return (key >= begin) & (key <= token)
+
+    loads["x"].wait()
+    loads["w_key"].wait()
+    loads["w_value"].wait()
+    for t in tiles:
+        x = f32(r.x[t, :])
+        a = bf16(x * inverse_rms(x) * r.norm_in[...])
+        r.a[t, :] = a
+        kp = dot(a, r.w_first[:, wide_k])
+        r.kp[t, :] = kp
+        k = turn(kp * inverse_rms(kp) * r.key_gain[...], r.cosine[t, :], r.sine[t, :])
+        r.kv[place, t, 0:head] = bf16(k)
+        r.kv[place, t, head : 2 * head] = bf16(dot(a, r.w_first[:, wide_v]))
+
+    def send_kv(source, route):
+        peer = peers["up"] if route == 0 else peers["y"]
+        return pltpu.make_async_remote_copy(
+            src_ref=r.kv.at[source],
+            dst_ref=r.kv.at[source],
+            send_sem=r.kv_send.at[route, source],
+            recv_sem=r.kv_recv.at[source],
+            device_id=peer,
+            device_id_type=MESH,
+        )
+
+    pl.when(z < last)(lambda: send_kv(place, 0).start())
+    pl.when(y == 0)(lambda: send_kv(place, 1).start())
+
+    loads["w_query"].wait()
+    for h in range(heads):
+        for t in tiles:
+            qp = dot(r.a[t, :], r.w_first[:, h * head : (h + 1) * head])
+            r.qp[t, h * head : (h + 1) * head] = qp
+            q = turn(qp * inverse_rms(qp) * r.query_gain[...], r.cosine[t, :], r.sine[t, :])
+            q = bf16(q * (scale * LOG2E))
+            r.q[h * rows + t.start : h * rows + t.stop, :] = q
+            r.qt[:, h * rows + t.start : h * rows + t.stop] = q.T
+
+    def visit(source, first):
+        vt = r.kv[source, :, head : 2 * head].T
+
+        def one_head(h, carry):
+            here = pl.ds(pl.multiple_of(h * rows, 128), rows)
+            for t in tiles:
+                s = dot(r.kv[source, t, 0:head], r.qt[:, here])
+                p = jnp.where(allowed(source, t.start, tile), jnp.exp2(s), 0.0)
+                total = jnp.sum(p, axis=0, keepdims=True)
+                if first and t.start == 0:
+                    r.total[:, here] = total
+                else:
+                    r.total[:, here] = r.total[:, here] + total
+                r.pt[t, :] = bf16(p)
+            o = dot(vt, r.pt[...])
+            r.ot[:, here] = o if first else r.ot[:, here] + o
+            return carry
+
+        lax.fori_loop(0, heads, one_head, 0)
+
+    visit(place, True)
+
+    @pl.when(y == 1)
+    def _():
+        send_kv(place - 1, 1).wait_recv()
+        visit(place - 1, False)
+
+    for back in range(1, z_count):
+
+        @pl.when(back <= z)
+        def _():
+            mine = place - 2 * back
+            other = mine + 1 - 2 * y
+            send_kv(mine, 0).wait_recv()
+            pl.when(z < last)(lambda: send_kv(mine, 0).start())
+            send_kv(mine, 1).start()
+            visit(mine, False)
+            send_kv(other, 1).wait_recv()
+            visit(other, False)
+
+    for h in range(heads):
+        here = slice(h * rows, (h + 1) * rows)
+        total = r.total[:, here]
+        o = r.ot[:, here] * (1.0 / total)
+        r.lse[:, here] = jnp.log2(total)
+        r.ot[:, here] = o
+        r.ob[:, h * head : (h + 1) * head] = bf16(o).T
+
+    loads["w_out"].wait()
+    for t in tiles:
+        ap = dot(r.ob[t, 0:joined], r.w_out[...])
+        r.ap[t, :] = ap
+        x1 = f32(r.x[t, :]) + ap * inverse_rms(ap) * r.norm_attn[...]
+        r.x1[t, :] = x1
+        m = bf16(x1 * inverse_rms(x1) * r.norm_pre[...])
+        r.m[t, :] = m
+        r.mt[:, t] = m.T
+    loads["w_gate"].wait()
+    loads["w_up"].wait()
+    block = hidden // 8
+
+    def feed(j, carry):
+        cols = pl.ds(pl.multiple_of(j * block, 128), block)
+        for t in tiles:
+            gate = dot(r.m[t, :], r.w_gate[:, cols])
+            up = dot(r.m[t, :], r.w_up[:, cols])
+            inner = 0.7978845608028654 * (gate + 0.044715 * gate * gate * gate)
+            th = jnp.tanh(inner)
+            cdf = 0.5 * (1.0 + th)
+            act = gate * cdf
+            slope = cdf + 0.5 * gate * (1.0 - th * th) * 0.7978845608028654 * (1.0 + 3 * 0.044715 * gate * gate)
+            r.hid[t, cols] = bf16(act * up)
+            r.side_gate[t, cols] = bf16(slope * up)
+            r.side_up[t, cols] = bf16(act)
+        return carry
+
+    lax.fori_loop(0, 8, feed, 0)
+    loads["w_down"].wait()
+    loads["dy"].wait()
+    r.gains[...] = jnp.zeros_like(r.gains)
+
+    def gain(k, terms):
+        r.gains[k, :, 0 : terms.shape[1]] = r.gains[k, :, 0 : terms.shape[1]] + terms
+
+    for t in tiles:
+        f = dot(r.hid[t, :], r.w_down[...])
+        inverse = inverse_rms(f)
+        dy = f32(r.dy[t, :])
+        r.out[t, :] = bf16(r.x1[t, :] + f * inverse * r.norm_post[...])
+        df, g = rms_back(f, inverse, r.norm_post[...], dy)
+        r.df[t, :] = bf16(df)
+        gain(3, g)
+
+    def down_grad(j, carry):
+        cols = pl.ds(pl.multiple_of(j * block, 128), block)
+        r.g_down[j] = bf16(dot(r.hid[:, cols].T, r.df[...]))
+        return carry
+
+    lax.fori_loop(0, 8, down_grad, 0)
+
+    chunks, number = {}, 0
+    sems = (r.red_send, r.red_recv, r.red_local)
+    for name, count in r_plan(sizes):
+        grad, total = r["g_" + name], r["t_" + name]
+        step = grad.shape[1] // count
+        chunks[name] = []
+        for i in range(count):
+            landing = tuple(r[f"land{k}_{name}"].at[i] for k in range(3))
+            first = "x" if i % 2 == 0 else "y"
+            chunks[name].append(Chunk(number, grad, total, i * step, step, first, landing, sems, me, peers, z_count))
+            number += 1
+    reducer = Reducer()
+    reducer.add(*chunks["down"])
+    reducer.tick()
+
+    def feed_back(j, carry):
+        cols = pl.ds(pl.multiple_of(j * block, 128), block)
+        for t in tiles:
+            dh = dot_nt(r.df[t, :], r.w_down[cols, :])
+            r.side_gate[t, cols] = bf16(dh * f32(r.side_gate[t, cols]))
+            r.side_up[t, cols] = bf16(dh * f32(r.side_up[t, cols]))
+        r.g_gate[j] = bf16(dot(r.mt[...], r.side_gate[:, cols]))
+        r.g_up[j] = bf16(dot(r.mt[...], r.side_up[:, cols]))
+        return carry
+
+    lax.fori_loop(0, 8, feed_back, 0)
+    reducer.add(*chunks["gate"], *chunks["up"])
+    reducer.tick()
+    for t in tiles:
+        dm = dot_nt(r.side_gate[t, :], r.w_gate[...]) + dot_nt(r.side_up[t, :], r.w_up[...])
+        x1 = r.x1[t, :]
+        dx1, g = rms_back(x1, inverse_rms(x1), r.norm_pre[...], dm)
+        gain(2, g)
+        dx1 = dx1 + f32(r.dy[t, :])
+        r.x1[t, :] = dx1
+        ap = r.ap[t, :]
+        dap, g = rms_back(ap, inverse_rms(ap), r.norm_attn[...], dx1)
+        gain(1, g)
+        r.dap[t, :] = bf16(dap)
+    reducer.tick()
+    for h in range(heads):
+        here = slice(h * rows, (h + 1) * rows)
+        wide = slice(h * head, (h + 1) * head)
+        ot = r.ot[:, here]
+        g = bf16(dot(bf16(ot), r.dap[...]))
+        r.g_out[2 * h] = g[0:half]
+        r.g_out[2 * h + 1] = g[half:head]
+        do = bf16(dot_nt(r.dap[...], r.w_out[wide, :]))
+        r.do[here, :] = do
+        dot_rows = do.T
+        r.dot[:, here] = dot_rows
+        r.delta[:, here] = jnp.sum(f32(dot_rows) * ot, axis=0, keepdims=True)
+    reducer.add(*chunks["out"])
+
+    r.ot[...] = jnp.zeros_like(r.ot)
+
+    def visit_back(source, target):
+        r.dkv[...] = jnp.zeros_like(r.dkv)
+        kt = r.kv[source, :, 0:head].T
+
+        def one_head(h, carry):
+            here = pl.ds(pl.multiple_of(h * rows, 128), rows)
+            for t in tiles:
+                s = dot(r.kv[source, t, 0:head], r.qt[:, here])
+                p = jnp.where(allowed(source, t.start, tile), jnp.exp2(s - r.lse[:, here]), 0.0)
+                dp = dot(r.kv[source, t, head : 2 * head], r.dot[:, here])
+                ds = bf16(p * (dp - r.delta[:, here]))
+                r.pt[t, :] = ds
+                r.dkv[t, 0:head] = r.dkv[t, 0:head] + dot(ds, r.q[here, :])
+                r.dkv[t, head : 2 * head] = r.dkv[t, head : 2 * head] + dot(bf16(p), r.do[here, :])
+            r.ot[:, here] = r.ot[:, here] + dot(kt, r.pt[...])
+            return carry
+
+        lax.fori_loop(0, heads, one_head, 0)
+        target[...] = bf16(r.dkv[...])
+
+    def stage_y(row):
+        return r.w_gate.at[0:rows, row * 2 * head : (row + 1) * 2 * head]
+
+    def stage_z(row):
+        return r.w_up.at[0:rows, row * 2 * head : (row + 1) * 2 * head]
+
+    def to_partner(row):
+        return pltpu.make_async_remote_copy(
+            src_ref=stage_y(row),
+            dst_ref=r.from_partner.at[row],
+            send_sem=r.dkv_send.at[0, row],
+            recv_sem=r.dkv_recv.at[0, row],
+            device_id=peers["y"],
+            device_id_type=MESH,
+        )
+
+    def to_below(row):
+        return pltpu.make_async_remote_copy(
+            src_ref=stage_z(row),
+            dst_ref=r.from_above.at[row],
+            send_sem=r.dkv_send.at[1, row],
+            recv_sem=r.dkv_recv.at[1, row],
+            device_id=peers["down"],
+            device_id_type=MESH,
+        )
+
+    def pass_down(row):
+        @pl.when(row < z)
+        def _():
+            to_partner(row).wait_recv()
+            pl.when(z < last)(lambda: to_below(row).wait_recv())
+            for t in tiles:
+                value = f32(stage_z(row)[t, :]) + f32(r.from_partner[row, t, :])
+                above = jnp.where(z < last, f32(r.from_above[row, t, :]), 0.0)
+                stage_z(row)[t, :] = bf16(value + above)
+            to_below(row).start()
+
+    for row in range(z_count):
+
+        @pl.when((row < z) | ((row == z) & (y == 1)))
+        def _():
+            visit_back(2 * row + 1 - y, stage_y(row))
+            to_partner(row).start()
+
+        reducer.tick()
+
+        @pl.when(row <= z)
+        def _():
+            visit_back(2 * row + y, stage_z(row))
+
+        if row > 0:
+            pass_down(row - 1)
+        reducer.tick()
+
+    for h in range(heads):
+        wide = slice(h * head, (h + 1) * head)
+        for t in tiles:
+            dq = (r.ot[:, h * rows + t.start : h * rows + t.stop] * scale).T
+            qp = r.qp[t, wide]
+            inverse = inverse_rms(qp)
+            dqp, g = rms_back(qp, inverse, r.query_gain[...], turn_back(dq, r.cosine[t, :], r.sine[t, :]))
+            gain(4, g)
+            r.ob[t, wide] = bf16(dqp)
+    for t in tiles:
+        r.at[:, t] = r.a[t, :].T
+    for p in range(4):
+        g = bf16(dot(r.at[...], r.ob[:, p * head : (p + 1) * head]))
+        r.g_query[2 * p] = g[:, 0:half]
+        r.g_query[2 * p + 1] = g[:, half:head]
+    reducer.add(*chunks["query"])
+    reducer.tick()
+
+    row_total = r.dkv
+
+    for row in range(z_count):
+
+        @pl.when(row == z)
+        def _():
+            pl.when(y == 0)(lambda: to_partner(row).wait_recv())
+            pl.when(z < last)(lambda: to_below(row).wait_recv())
+            for t in tiles:
+                beside = jnp.where(y == 0, f32(r.from_partner[row, t, :]), 0.0)
+                above = jnp.where(z < last, f32(r.from_above[row, t, :]), 0.0)
+                row_total[t, :] = f32(stage_z(row)[t, :]) + beside + above
+
+    for t in tiles:
+        dk = r.dkv[t, 0:head] * LN2
+        kp = r.kp[t, :]
+        dkp, g = rms_back(kp, inverse_rms(kp), r.key_gain[...], turn_back(dk, r.cosine[t, :], r.sine[t, :]))
+        gain(5, g)
+        r.ob[t, wide_k] = bf16(dkp)
+        r.ob[t, wide_v] = bf16(r.dkv[t, head : 2 * head])
+        da = dot_nt(r.ob[t, :], r.w_first[...])
+        x = f32(r.x[t, :])
+        dx, g = rms_back(x, inverse_rms(x), r.norm_in[...], da)
+        gain(0, g)
+        r.dx[t, :] = bf16(r.x1[t, :] + dx)
+    low = width // 2
+    for upper in range(2):
+        g = bf16(dot(r.at[upper * low : (upper + 1) * low, :], r.ob[:, joined : joined + 2 * head]))
+        for p in range(4):
+            which, side = p // 2, p % 2
+            r.g_kv[4 * which + 2 * upper + side] = g[:, p * half : (p + 1) * half]
+    r.g_gain[...] = jnp.zeros_like(r.g_gain)
+    at = 0
+    for k, size in enumerate((width, width, width, width, head, head)):
+        g = jnp.sum(r.gains[k], axis=0, keepdims=True)
+        for part in range(size // 128):
+            r.g_gain[at // 16, at % 16 : at % 16 + 1, :] = g[:, part * 128 : (part + 1) * 128]
+            at += 1
+    reducer.add(*chunks["kv"], *chunks["gain"])
+    reducer.finish()
+
+    pl.when(z < last)(lambda: send_kv(place, 0).wait_send())
+    pl.when(y == 0)(lambda: send_kv(place, 1).wait_send())
+    for back in range(1, z_count):
+
+        @pl.when(back <= z)
+        def _():
+            mine = place - 2 * back
+            pl.when(z < last)(lambda: send_kv(mine, 0).wait_send())
+            send_kv(mine, 1).wait_send()
+
+    for row in range(z_count):
+        pl.when((row < z) | ((row == z) & (y == 1)))(lambda: to_partner(row).wait_send())
+        pl.when(row < z)(lambda: to_below(row).wait_send())
+
+
+def r_plan(sizes):
+    return [("down", 2), ("gate", 2), ("up", 2), ("out", 2), ("query", 2), ("kv", 2), ("gain", 1)]
+
+
+def gradient_shapes(sizes):
+    rows, width, hidden, heads, head, z_count = sizes
+    joined, half = heads * head, head // 2
+    return {
+        "down": ((8, hidden // 8, width), (8, hidden // 8, width)),
+        "gate": ((8, width, hidden // 8), (width, hidden)),
+        "up": ((8, width, hidden // 8), (width, hidden)),
+        "out": ((8, joined // 8, width), (8, joined // 8, width)),
+        "query": ((8, width, joined // 8), (width, joined)),
+        "kv": ((8, width // 2, half), (2, 2, width // 2, head)),
+        "gain": ((8, 16, 128), (8, 16, 128)),
+    }
+
+
+def layer_scratch(sizes):
+    rows, width, hidden, heads, head, z_count = sizes
+    joined = heads * head
+    low, wide = jnp.bfloat16, jnp.float32
+    arrays = {
+        "x": ((rows, width), low),
+        "w_first": ((width, joined + 2 * head), low),
+        "w_out": ((joined, width), low),
+        "w_gate": ((width, hidden), low),
+        "w_up": ((width, hidden), low),
+        "w_down": ((hidden, width), low),
+        "dy": ((rows, width), low),
+        "a": ((rows, width), low),
+        "at": ((width, rows), low),
+        "gains": ((6, 8, width), wide),
+        "kp": ((rows, head), wide),
+        "kv": ((2 * z_count, rows, 2 * head), low),
+        "qp": ((rows, joined), wide),
+        "q": ((heads * rows, head), low),
+        "qt": ((head, heads * rows), low),
+        "pt": ((rows, rows), low),
+        "ot": ((head, heads * rows), wide),
+        "total": ((1, heads * rows), wide),
+        "lse": ((1, heads * rows), wide),
+        "delta": ((1, heads * rows), wide),
+        "ob": ((rows, joined + 2 * head), low),
+        "ap": ((rows, width), wide),
+        "x1": ((rows, width), wide),
+        "m": ((rows, width), low),
+        "mt": ((width, rows), low),
+        "hid": ((rows, hidden), low),
+        "side_gate": ((rows, hidden), low),
+        "side_up": ((rows, hidden), low),
+        "df": ((rows, width), low),
+        "dap": ((rows, width), low),
+        "do": ((heads * rows, head), low),
+        "dot": ((head, heads * rows), low),
+        "dkv": ((rows, 2 * head), wide),
+        "from_partner": ((z_count, rows, 2 * head), low),
+        "from_above": ((z_count, rows, 2 * head), low),
+    }
+    shapes = gradient_shapes(sizes)
+    pieces = 0
+    for name, count in r_plan(sizes):
+        (eight, high, columns), kind = shapes[name][0], wide if name == "gain" else low
+        step = high // count
+        pieces += count
+        arrays["g_" + name] = (shapes[name][0], kind)
+        arrays["land0_" + name] = ((count, 4, step, columns), kind)
+        arrays["land1_" + name] = ((count, 2, step, columns), kind)
+        arrays["land2_" + name] = ((count, 1, 2 * step, columns), kind)
+    sems = {
+        "load_sem": (9,),
+        "kv_send": (2, 2 * z_count),
+        "kv_recv": (2 * z_count,),
+        "dkv_send": (2, z_count),
+        "dkv_recv": (2, z_count),
+        "red_send": (pieces, STAGES),
+        "red_recv": (pieces, STAGES),
+        "red_local": (pieces,),
+    }
+    return arrays, sems
+
+
+def layer_bytes(sizes):
+    total = 0
+    for shape, kind in layer_scratch(sizes)[0].values():
+        size = jnp.dtype(kind).itemsize
+        for n in shape[:-2]:
+            size *= n
+        total += size * max(shape[-2], 8) * max(shape[-1], 128)
+    return total
+
+
+VMEM_BYTES = 64 * 2**20
+
+
+def whole_layer(sizes, tokens, lengths, cotangent, norm_in, w_query, w_key, w_value, query_gain, key_gain, w_out, norm_attn, norm_pre, w_gate, w_up, w_down, norm_post):
+    rows, width, hidden, heads, head, z_count = sizes
+    place = lax.axis_index("blk")
+    seg, pos = segment_of(place * rows + jnp.arange(rows, dtype=jnp.int32), lengths[0])
+    cosine, sine = rotary_tables(pos, head)
+    inputs = {
+        "lengths": lengths,
+        "cosine": cosine,
+        "sine": sine,
+        "norm_in": norm_in[None],
+        "query_gain": query_gain[None],
+        "key_gain": key_gain[None],
+        "norm_attn": norm_attn[None],
+        "norm_pre": norm_pre[None],
+        "norm_post": norm_post[None],
+        "x_in": tokens[0],
+        "w_key_in": w_key,
+        "w_value_in": w_value,
+        "w_query_in": w_query,
+        "w_out_in": w_out,
+        "w_gate_in": w_gate,
+        "w_up_in": w_up,
+        "w_down_in": w_down,
+        "dy_in": cotangent[0],
+    }
+    spaces = {name: pltpu.SMEM if name == "lengths" else pl.ANY if name.endswith("_in") and name != "norm_in" else pltpu.VMEM for name in inputs}
+    shapes = gradient_shapes(sizes)
+    outputs = {"out": (rows, width), "dx": (rows, width)}
+    outputs.update({"t_" + name: shapes[name][1] for name in shapes})
+    arrays, sems = layer_scratch(sizes)
+    names = list(inputs) + list(outputs) + list(arrays) + list(sems)
+    results = pl.pallas_call(
+        functools.partial(layer_kernel, sizes, names),
+        out_shape=tuple(
+            jax.ShapeDtypeStruct(shape, jnp.float32 if name == "t_gain" else jnp.bfloat16) for name, shape in outputs.items()
+        ),
+        in_specs=[pl.BlockSpec(memory_space=spaces[name]) for name in inputs],
+        out_specs=tuple(
+            pl.BlockSpec(memory_space=pl.ANY if name.startswith("t_") else pltpu.VMEM) for name in outputs
+        ),
+        scratch_shapes=[pltpu.VMEM(*item) for item in arrays.values()]
+        + [pltpu.SemaphoreType.DMA(item) for item in sems.values()],
+        compiler_params=pltpu.CompilerParams(
+            collective_id=1, has_side_effects=True, vmem_limit_bytes=VMEM_BYTES
+        ),
+    )(*inputs.values())
+    r = Names(zip(outputs, results, strict=True))
+    flat = r.t_gain.reshape(-1)
+    cuts, at = [], 0
+    for size in (width, width, width, width, head, head):
+        cuts.append(flat[at : at + size])
+        at += size
+    g_in, g_attn, g_pre, g_post, g_qgain, g_kgain = cuts
+    both = r.t_kv.reshape(2, width, head)
+    return (
+        r.out[None],
+        r.dx[None],
+        g_in,
+        f32(r.t_query),
+        f32(both[0]),
+        f32(both[1]),
+        g_qgain,
+        g_kgain,
+        f32(r.t_out.reshape(heads * head, width)),
+        g_attn,
+        g_pre,
+        f32(r.t_gate),
+        f32(r.t_up),
+        f32(r.t_down.reshape(hidden, width)),
+        g_post,
+    )
+
+
 def per_device(
     tokens,
     lengths,
@@ -475,6 +1103,27 @@
     rows = tokens.shape[1]
     head = query_gain.shape[0]
     heads = w_query.shape[1] // head
+    sizes = (rows, tokens.shape[2], w_gate.shape[1], heads, head, lax.axis_size("blk") // 2)
+    if layer_bytes(sizes) <= VMEM_BYTES:
+        return whole_layer(
+            sizes,
+            tokens,
+            lengths,
+            cotangent,
+            norm_in,
+            w_query,
+            w_key,
+            w_value,
+            query_gain,
+            key_gain,
+            w_out,
+            norm_attn,
+            norm_pre,
+            w_gate,
+            w_up,
+            w_down,
+            norm_post,
+        )
     scale = head ** (-0.5)
     count = lax.axis_size("blk")
     place = lax.axis_index("blk")

time: 631 us -> 276 us (0.44); the launches traced: 622 us -> 276 us
  starting transfers between devices: 104 us -> 0 us
  matrix products: 103 us -> 0 us
  local copies, waits for them, and re-layouts: 106 us -> 10.6 us
  waiting for transfers between devices: 70 us -> 0 us
  Pallas kernels: 185 us -> 247 us
  other arithmetic: 51 us -> 17.1 us
    ppermute x22 -> x0, starting transfers between devices: 104 us -> none  [the longest x14 77.8 us: from_behind(): return lax.ppermute(block, axis, route)]
    dot_general x76 -> x0, matrix products: 103 us -> none  [the longest x8 19.6 us: absorb(): jnp.einsum('hqk,kd->hqd', expo.astype(jnp.bfloat16), pair[1], preferred_e...]
    ppermute x22 -> x0, waiting for transfers between devices: 70 us -> none  [the longest x14 53.4 us: from_behind(): return lax.ppermute(block, axis, route)]
    pallas_call x1, Pallas kernels: 185 us -> 247 us  [whole_layer(): pl.pallas_call(functools.partial(layer_kernel, sizes, names), out_shape=t...]
    while x66 -> x0, local copies, waits for them, and re-layouts: 32.2 us -> none
    unnamed x168 -> x16, local copies, waits for them, and re-layouts: 29 us -> 1.58 us
    convert_element_type x4 -> x0, local copies, waits for them, and re-layouts: 17.6 us -> none  [columns_to_panels(): jnp.transpose(value.reshape(rows, 8, columns // 8), (1, 0, 2))]
    reshape x4 -> x0, local copies, waits for them, and re-layouts: 15.7 us -> none  [the longest x3 14.1 us: panels_to_columns(): jnp.transpose(panels.astype(jnp.float32), (1, 0, 2))]
  transfers between devices with their start and end apart: 22 -> 0, of which waited for: 21 -> 0; matrix products, arithmetic and copies ran while one was open for 12% -> 0% of each run, Pallas kernels for 0% -> 0%
where the time goes in v2:
time: 276 us
  Pallas kernels  247 us (89%)
  other arithmetic  17.1 us (6%)
  local copies, waits for them, and re-layouts  10.6 us (4%)
    pallas_call x1, Pallas kernels, whole_layer(): pl.pallas_call(functools.partial(layer_kernel, sizes, names), out_shape=t...  247 us
    convert_element_type x6, other arithmetic, f32(): return value.astype(jnp.float32)  13.9 us

profile of v2, /device:TPU:0, one launch (start us, length us, event | category | flops | bytes accessed | tf_op | source)
XLA Modules:
  0.0 275.6 jit_solution(13967611867698287270)
XLA Ops:
  0.7 0.8 reduce-window.4
  1.5 0.1 convert_reduce_fusion
  1.6 0.7 fusion
  2.2 0.1 select_reduce_fusion
  2.3 1.5 multiply_sine_fusion
  3.9 1.3 broadcast_in_dim.48.refs_3_
  5.1 1.3 broadcast_in_dim.51.refs_6_
  6.4 1.3 broadcast_in_dim.52.refs_7_
  7.7 1.3 broadcast_in_dim.53.refs_8_
  8.9 247.2 %shard_map.271 = (bf16[384,640]{1,0:T(8,128)(2,1)}, bf16[384,640]{1,0:T(8,128)(2,1)}, bf16[8,256,640]{2,1,0:T(8,128)(2,1)}, bf16[640,2048]{1,0:T(8,128)(2,1)}, b...) custom-call(s32[1,4]{1,0:T(1,128)} %refs_0_.1, ...), custom_call_target="tpu_custom_call" | custom-call | tf_op jit(solution)/shard_map/pallas_call | solution.py:1043
  256.2 0.0 copy-start.2
  256.2 1.3 fusion.1
  257.4 1.2 bitcast_convert_fusion.2
  258.6 1.4 fusion.2
  260.0 1.3 fusion.3
  261.4 2.9 %bitcast_convert_fusion = f32[2048,640]{1,0:T(8,128)} fusion(bf16[8,256,640]{2,1,0:T(8,128)(2,1)S(1)} %copy-done.2), kind=kLoop, calls=%fused_computation | loop fusion | flops 1310720 | bytes 7864320 | tf_op jit(solution)/shard_map/convert_element_type | solution.py:513
  264.3 0.0 copy-done.1
  264.3 3.1 %convert_element_type.52 = f32[640,2048]{1,0:T(8,128)} convert(bf16[640,2048]{1,0:T(8,128)(2,1)S(1)} %copy-done.1) | non-fusion elementwise | flops 1310720 | bytes 7864320 | tf_op jit(solution)/shard_map/convert_element_type | solution.py:513
  267.4 3.1 %convert_element_type.53 = f32[640,2048]{1,0:T(8,128)} convert(bf16[640,2048]{1,0:T(8,128)(2,1)S(1)} %copy-done) | non-fusion elementwise | flops 1310720 | bytes 7864320 | tf_op jit(solution)/shard_map/convert_element_type | solution.py:513
  270.5 0.0 copy-done.4
  270.5 1.8 bitcast_convert_fusion.1
  272.3 1.8 convert_element_type.45
  274.1 0.8 copy.33
  274.9 0.8 copy.34
  (14 shorter events, 0.0 us)
Async XLA Ops:
  256.2 5.2 %copy-start.2 = (bf16[8,256,640]{2,1,0:T(8,128)(2,1)S(1)}, bf16[8,256,640]{2,1,0:T(8,128)(2,1)}, u32[]{:S(2)}) copy-start(bf16[8,256,640]{2,1,0:T(8,128)(2,1)} %get-tuple-element.32) | copy-start | bytes 7864324
  261.4 2.9 %copy-start.1 = (bf16[640,2048]{1,0:T(8,128)(2,1)S(1)}, bf16[640,2048]{1,0:T(8,128)(2,1)}, u32[]{:S(2)}) copy-start(bf16[640,2048]{1,0:T(8,128)(2,1)} %get-tuple-element.30) | copy-start | bytes 7864324
  264.3 3.1 %copy-start = (bf16[640,2048]{1,0:T(8,128)(2,1)S(1)}, bf16[640,2048]{1,0:T(8,128)(2,1)}, u32[]{:S(2)}) copy-start(bf16[640,2048]{1,0:T(8,128)(2,1)} %get-tuple-element.31) | copy-start | bytes 7864324
  267.4 3.1 %copy-start.4 = (bf16[8,128,640]{2,1,0:T(8,128)(2,1)S(1)}, bf16[8,128,640]{2,1,0:T(8,128)(2,1)}, u32[]{:S(2)}) copy-start(bf16[8,128,640]{2,1,0:T(8,128)(2,1)} %get-tuple-element.29) | copy-start | bytes 3932164
  270.5 1.8 copy-start.3
  272.2 1.8 copy-start.6
  272.2 2.6 copy-start.5
